TPU v7x, 32 devices: a whole 2x2x4 slice. The times are simulated.
32 devices in a mesh: row: 16 (over z, x, core), col: 2 (over y).
Axes of the slice: x: 2, y: 2, z: 4, core: 2. Of those that a mesh axis runs over, the one named last changes fastest.
Arguments:
- start_vectors: float32 [16384, 256], P('row', 'col'), may hold values from -6 to 6
- ham_blocks: float32 [128, 8, 128, 128], P(('row', 'col')), may hold values from -0.1875 to 0.1875
- block_cols: int32 [128, 8], P(('row', 'col')), may hold values from 0 to 127, as said below
- block_counts: int32 [128], P(('row', 'col')), may hold values from 1 to 8, as said below
- check_weights: float32 [256], replicated, may hold values from -0.375 to 0.375
Outputs:
- filtered: float32 [16384, 256], P('row', 'col')
- checksum: float32 [16384], P(('row', 'col'))
Inputs may be any that keep to these rules, and one draw needn't show every extreme that they name: `block_cols`: slot j of block row b names block column (b + d) mod 128 for offsets d that are distinct within the row and lie from -4 to 3; slot 0 names the block row itself (d = 0). Only the first block_counts[b] slots of block row b are part of the operator. The block rows of one thirty-second of the devices (at least one device) hold 8 live slots each, all block rows of such a device alike; every other block row holds 1 to 3.
All inputs are finite; a program needn't handle non-finite values.
Results may differ from a plain program's by a relative error of at most 0.0003.
Values sent between devices are 32-bit elements; how exact they have to be, the bound alone decides.
A program may use at most 64 MiB of HBM per device.

v0:
```python
import jax
import jax.numpy as jnp
from jax import lax
from jax.sharding import PartitionSpec as P

REACH = 4
ITERS = 3


CENTRE = 0.25
HALF_WIDTH = 1.5
HIGHEST_PRECISION = lax.Precision.HIGHEST


def shifted_2(value, axis, steps):
    count = lax.axis_size(axis)
    pairs = [(source, (source + steps) % count) for source in range(count)]
    return lax.ppermute(value, axis, pairs)


def accumulate(ham_blocks, block_cols, finishes, window, window_check, base_block, total_blocks):
    block_size = ham_blocks.shape[2]
    vector_width = window.shape[1]
    results = []
    result_checks = []
    for row_index in range(ham_blocks.shape[0]):
        matrices = ham_blocks[row_index]
        columns = block_cols[row_index]

        def add_block(slot_index, carried, matrices=matrices, columns=columns):
            summed, summed_check = carried
            offset = jnp.mod(columns[slot_index] - base_block, total_blocks) * block_size
            segment = lax.dynamic_slice_in_dim(window, offset, block_size, 0)
            segment_check = lax.dynamic_slice_in_dim(window_check, offset, block_size, 0)
            matrix = lax.dynamic_index_in_dim(matrices, slot_index, 0, keepdims=False)
            summed = summed + jnp.dot(
                matrix, segment, precision=HIGHEST_PRECISION, preferred_element_type=jnp.float32
            )
            summed_check = summed_check + jnp.dot(
                matrix,
                segment_check,
                precision=HIGHEST_PRECISION,
                preferred_element_type=jnp.float32,
            )
            return (summed, summed_check)

        initial = (
            jnp.zeros((block_size, vector_width), jnp.float32),
            jnp.zeros((block_size,), jnp.float32),
        )
        summed, summed_check = lax.fori_loop(0, finishes[row_index], add_block, initial)
        results.append(summed)
        result_checks.append(summed_check)
    return (jnp.concatenate(results, 0), jnp.concatenate(result_checks, 0))


def near_window(vectors, checks, reach_devices):
    pieces = []
    piece_checks = []
    for distance in range(-reach_devices, reach_devices + 1):
        if distance == 0:
            pieces.append(vectors)
            piece_checks.append(checks)
        else:
            shifted, shifted_check = shifted_2((vectors, checks), ("row", "col"), -distance)
            pieces.append(shifted)
            piece_checks.append(shifted_check)
    return (jnp.concatenate(pieces, 0), jnp.concatenate(piece_checks, 0))


def per_device(start_vectors, ham_blocks, block_cols, block_counts, check_weights):
    row_vectors = lax.all_to_all(start_vectors, "col", split_axis=0, concat_axis=1, tiled=True)
    checks = jnp.dot(
        row_vectors, check_weights, precision=HIGHEST_PRECISION, preferred_element_type=jnp.float32
    )
    blocks_here = ham_blocks.shape[0]
    total_blocks = lax.axis_size(("row", "col")) * blocks_here
    position = lax.axis_index(("row", "col"))
    neighbours = (REACH + blocks_here - 1) // blocks_here
    base_block = (position - neighbours) * blocks_here

    def apply_operator(vectors, vector_checks):
        window, window_check = near_window(vectors, vector_checks, neighbours)
        return accumulate(
            ham_blocks, block_cols, block_counts, window, window_check, base_block, total_blocks
        )

    previous, previous_check = (row_vectors, checks)
    image_rows, image_check = apply_operator(row_vectors, checks)
    current = (image_rows - CENTRE * row_vectors) / HALF_WIDTH
    current_check = (image_check - CENTRE * checks) / HALF_WIDTH
    for step_index in range(ITERS - 1):
        image_rows, image_check = apply_operator(current, current_check)
        following = 2.0 * (image_rows - CENTRE * current) / HALF_WIDTH - previous
        following_check = 2.0 * (image_check - CENTRE * current_check) / HALF_WIDTH - previous_check
        previous, previous_check = (current, current_check)
        current, current_check = (following, following_check)
    filtered = lax.all_to_all(current, "col", split_axis=1, concat_axis=0, tiled=True)
    return (filtered, current_check)


def solution(mesh):
    placed = (
        P("row", "col"),
        P(("row", "col"), None, None, None),
        P(("row", "col"), None),
        P(("row", "col")),
        P(),
    )
    return jax.shard_map(
        per_device,
        mesh=mesh,
        in_specs=placed,
        out_specs=(P("row", "col"), P(("row", "col"))),
        check_vma=False,
    )
```

profile of v0, /device:TPU:27, one launch (start us, length us, event | category | flops | bytes accessed | tf_op | source)
XLA Modules:
  0.0 503.4 jit_solution(3688012039442352217)
XLA Ops:
  0.6 3.5 all-to-all-start
  4.2 1.7 slice_bitcast_fusion.3
  5.9 5.6 %all-to-all-done = f32[2,512,128]{2,1,0:T(8,128)S(1)} async-done(((f32[2,512,128]{2,1,0:T(8,128)}), f32[2,512,128]{2,1,0:T(8,128)S(1)}, u32[]{:S(2)}, u32[]{:S(2)}) %all-to-all-start) | async-done | bytes 524320 | tf_op jit(solution)/shard_map/all_to_all | solution.py:72
  13.0 2.0 collective-permute-start.2
  15.0 1.5 collective-permute-start.1
  17.1 12.6 %collective-permute-done.2 = f32[512]{0:T(512)S(1)} collective-permute-done((f32[512]{0:T(512)S(1)}, f32[512]{0:T(512)S(1)}, u32[]{:S(2)}, u32[]{:S(2)}) %collective-permute-start.2) | collective-permute-done | bytes 2080 | tf_op jit(solution)/shard_map/ppermute | solution.py:18
  30.8 4.2 collective-permute-done.1
  37.3 27.6 %while.168 = (s32[]{:T(128)}, f32[128,256]{1,0:T(8,128)S(1)}, f32[128]{0:T(128)S(1)}, s32[]{:T(128)}, f32[8,128,128]{2,1,0:T(8,128)S(1)}, /*index=5*/s32[8]{0:T(...) while((s32[]{:T(128)}, f32[128,256]{1,0:T(8,128)S(1)}, ...), condition=%wide.region_1.2_spmd, body=%wide.region_0.1_spmd.sunk | while | flops 50561172 | bytes 526194 | solution.py:51
  65.0 31.6 %while.169 = (s32[]{:T(128)}, f32[128,256]{1,0:T(8,128)S(1)}, f32[128]{0:T(128)S(1)}, s32[]{:T(128)}, f32[8,128,128]{2,1,0:T(8,128)S(1)}, /*index=5*/s32[8]{0:T(...) while((s32[]{:T(128)}, f32[128,256]{1,0:T(8,128)S(1)}, ...), condition=%wide.region_3.4_spmd, body=%wide.region_2.3_spmd.sunk | while | flops 50561172 | bytes 526194 | solution.py:51
  96.6 26.2 %while.170 = (s32[]{:T(128)}, f32[128,256]{1,0:T(8,128)S(1)}, f32[128]{0:T(128)S(1)}, s32[]{:T(128)}, f32[8,128,128]{2,1,0:T(8,128)S(1)}, /*index=5*/s32[8]{0:T(...) while((s32[]{:T(128)}, f32[128,256]{1,0:T(8,128)S(1)}, ...), condition=%wide.region_5.6_spmd, body=%wide.region_4.5_spmd.sunk | while | flops 50561172 | bytes 526194 | solution.py:51
  123.3 28.3 %while.171 = (s32[]{:T(128)}, f32[128,256]{1,0:T(8,128)S(1)}, f32[128]{0:T(128)S(1)}, s32[]{:T(128)}, f32[8,128,128]{2,1,0:T(8,128)S(1)}, /*index=5*/s32[8]{0:T(...) while((s32[]{:T(128)}, f32[128,256]{1,0:T(8,128)S(1)}, ...), condition=%wide.region_7.8_spmd, body=%wide.region_6.7_spmd.sunk | while | flops 50561172 | bytes 526194 | solution.py:51
  152.3 1.7 collective-permute-start.7
  154.2 1.7 collective-permute-start.5
  157.4 13.7 %collective-permute-done.4 = f32[512,256]{1,0:T(8,128)S(1)} collective-permute-done((f32[512,256]{1,0:T(8,128)S(1)}, f32[512,256]{1,0:T(8,128)S(1)}, u32[]{:S(2)}, u32[]{:S(2)}) %collective-permute-start.4) | collective-permute-done | bytes 524320 | tf_op jit(solution)/shard_map/ppermute | solution.py:18
  171.0 6.1 %collective-permute-done.5 = f32[512,256]{1,0:T(8,128)S(1)} collective-permute-done((f32[512,256]{1,0:T(8,128)S(1)}, f32[512,256]{1,0:T(8,128)S(1)}, u32[]{:S(2)}, u32[]{:S(2)}) %collective-permute-start.5) | collective-permute-done | bytes 524320 | tf_op jit(solution)/shard_map/ppermute | solution.py:18
  179.0 38.1 %while.172 = (s32[]{:T(128)}, f32[128,256]{1,0:T(8,128)S(1)}, f32[128]{0:T(128)}, s32[]{:T(128)}, f32[8,128,128]{2,1,0:T(8,128)S(1)}, /*index=5*/s32[8]{0:T(128)...) while((s32[]{:T(128)}, f32[128,256]{1,0:T(8,128)S(1)}, ...), condition=%wide.region_9.10_spmd, body=%wide.region_8.9_spmd.sunk | while | flops 50561172 | bytes 526194 | solution.py:51
  182.2 1.5 fusion.235
  186.9 1.5 fusion.235
  191.6 1.5 fusion.235
  196.3 1.5 fusion.235
  200.9 1.5 fusion.235
  205.6 1.5 fusion.235
  210.3 1.5 fusion.235
  215.0 1.5 fusion.235
  217.8 41.5 %while.173 = (s32[]{:T(128)}, f32[128,256]{1,0:T(8,128)S(1)}, f32[128]{0:T(128)}, s32[]{:T(128)}, f32[8,128,128]{2,1,0:T(8,128)S(1)}, /*index=5*/s32[8]{0:T(128)...) while((s32[]{:T(128)}, f32[128,256]{1,0:T(8,128)S(1)}, ...), condition=%wide.region_11.12_spmd, body=%wide.region_10.11_spmd.sunk | while | flops 50561172 | bytes 526194 | solution.py:51
  259.8 39.8 %while.174 = (s32[]{:T(128)}, f32[128,256]{1,0:T(8,128)S(1)}, f32[128]{0:T(128)}, s32[]{:T(128)}, f32[8,128,128]{2,1,0:T(8,128)S(1)}, /*index=5*/s32[8]{0:T(128)...) while((s32[]{:T(128)}, f32[128,256]{1,0:T(8,128)S(1)}, ...), condition=%wide.region_13.14_spmd, body=%wide.region_12.13_spmd.sunk | while | flops 50561172 | bytes 526194 | solution.py:51
  300.8 47.6 %while.175 = (s32[]{:T(128)}, f32[128,256]{1,0:T(8,128)}, f32[128]{0:T(128)}, s32[]{:T(128)}, f32[8,128,128]{2,1,0:T(8,128)S(1)}, /*index=5*/s32[8]{0:T(128)}, s...) while((s32[]{:T(128)}, f32[128,256]{1,0:T(8,128)}, ...), condition=%wide.region_15.16_spmd, body=%wide.region_14.15_spmd.sunk | while | flops 50561172 | bytes 526194 | solution.py:51
  303.3 1.9 convolution_add_fusion.31
  305.2 1.4 fusion.250
  309.2 1.9 convolution_add_fusion.31
  311.1 1.4 fusion.250
  315.1 1.9 convolution_add_fusion.31
  316.9 1.4 fusion.250
  320.9 1.9 convolution_add_fusion.31
  326.8 1.9 convolution_add_fusion.31
  332.6 1.9 convolution_add_fusion.31
  338.5 1.9 convolution_add_fusion.31
  344.4 1.9 convolution_add_fusion.31
  349.2 1.7 collective-permute-start.11
  352.0 1.7 collective-permute-start.9
  353.8 15.0 %collective-permute-done.8 = f32[512,256]{1,0:T(8,128)S(1)} collective-permute-done((f32[512,256]{1,0:T(8,128)S(1)}, f32[512,256]{1,0:T(8,128)S(1)}, u32[]{:S(2)}, u32[]{:S(2)}) %collective-permute-start.8) | collective-permute-done | bytes 524320 | tf_op jit(solution)/shard_map/ppermute | solution.py:18
  368.9 6.1 %collective-permute-done.9 = f32[512,256]{1,0:T(8,128)S(1)} collective-permute-done((f32[512,256]{1,0:T(8,128)S(1)}, f32[512,256]{1,0:T(8,128)S(1)}, u32[]{:S(2)}, u32[]{:S(2)}) %collective-permute-start.9) | collective-permute-done | bytes 524320 | tf_op jit(solution)/shard_map/ppermute | solution.py:18
  376.3 32.3 %while.177 = (s32[]{:T(128)}, f32[128,256]{1,0:T(8,128)S(1)}, f32[128]{0:T(128)S(1)}, s32[]{:T(128)}, f32[8,128,128]{2,1,0:T(8,128)S(1)}, /*index=5*/s32[8]{0:T(...) while((s32[]{:T(128)}, f32[128,256]{1,0:T(8,128)S(1)}, ...), condition=%wide.region_19.20_spmd, body=%wide.region_18.19_spmd.sunk | while | flops 50561172 | bytes 526194 | solution.py:51
  408.6 28.3 %while.176 = (s32[]{:T(128)}, f32[128,256]{1,0:T(8,128)S(1)}, f32[128]{0:T(128)S(1)}, s32[]{:T(128)}, f32[8,128,128]{2,1,0:T(8,128)S(1)}, /*index=5*/s32[8]{0:T(...) while((s32[]{:T(128)}, f32[128,256]{1,0:T(8,128)S(1)}, ...), condition=%wide.region_17.18_spmd, body=%wide.region_16.17_spmd.sunk | while | flops 50561172 | bytes 526194 | solution.py:51
  437.0 28.3 %while.179 = (s32[]{:T(128)}, f32[128,256]{1,0:T(8,128)S(1)}, f32[128]{0:T(128)S(1)}, s32[]{:T(128)}, f32[8,128,128]{2,1,0:T(8,128)S(1)}, /*index=5*/s32[8]{0:T(...) while((s32[]{:T(128)}, f32[128,256]{1,0:T(8,128)S(1)}, ...), condition=%wide.region_23.24_spmd, body=%wide.region_22.23_spmd.sunk | while | flops 50561172 | bytes 526194 | solution.py:51
  465.4 27.2 %while.178 = (s32[]{:T(128)}, f32[128,256]{1,0:T(8,128)S(1)}, f32[128]{0:T(128)S(1)}, s32[]{:T(128)}, f32[8,128,128]{2,1,0:T(8,128)S(1)}, /*index=5*/s32[8]{0:T(...) while((s32[]{:T(128)}, f32[128,256]{1,0:T(8,128)S(1)}, ...), condition=%wide.region_21.22_spmd, body=%wide.region_20.21_spmd.sunk | while | flops 50561172 | bytes 526194 | solution.py:51
  493.7 3.5 all-to-all-start.1
  497.8 4.8 all-to-all-done.1
  (372 shorter events, 247.8 us)
Async XLA Ops:
  0.6 11.8 %copy-start = (f32[256]{0:T(256)S(1)}, f32[256]{0:T(256)}, u32[]{:S(2)}) copy-start(f32[256]{0:T(256)} %param.33) | copy-start | bytes 3076
  0.6 10.9 %all-to-all-start = ((f32[2,512,128]{2,1,0:T(8,128)}), f32[2,512,128]{2,1,0:T(8,128)S(1)}, u32[]{:S(2)}, u32[]{:S(2)}) async-start(f32[2,512,128]{2,1,0:T(8,128)} %bitcast.393), calls=%async_computation | async-start | bytes 1048576 | tf_op jit(solution)/shard_map/all_to_all | solution.py:72
  4.2 7.8 %copy-start.14 = (s32[4,8]{1,0:T(4,128)S(1)}, s32[4,8]{1,0:T(4,128)}, u32[]{:S(2)}) copy-start(s32[4,8]{1,0:T(4,128)} %param.31) | copy-start | bytes 388
  5.9 10.5 %copy-start.13 = (s32[4]{0:T(128)S(1)}, s32[4]{0:T(128)}, u32[]{:S(2)}) copy-start(s32[4]{0:T(128)} %param.32) | copy-start | bytes 52
  11.6 18.1 %collective-permute-start = (f32[512,256]{1,0:T(8,128)S(1)}, f32[512,256]{1,0:T(8,128)}, u32[]{:S(2)}, u32[]{:S(2)}) collective-permute-start(f32[512,256]{1,0:T(8,128)S(1)} %copy_bitcast_fusion), channel_id=1, source_target_pairs={{0,1},{1,2},{2,3},{3,4},{4,5},{5,6},{6,7},{7,8},{8,9},{9,10},{10,1... | collective-permute-start | bytes 1572872 | tf_op jit(solution)/shard_map/ppermute | solution.py:18
  13.0 16.7 %collective-permute-start.2 = (f32[512]{0:T(512)S(1)}, f32[512]{0:T(512)S(1)}, u32[]{:S(2)}, u32[]{:S(2)}) collective-permute-start(f32[512]{0:T(512)S(1)} %bitcast.394), channel_id=1, source_target_pairs={{0,1},{1,2},{2,3},{3,4},{4,5},{5,6},{6,7},{7,8},{8,9},{9,10},{10,1... | collective-permute-start | bytes 6152 | tf_op jit(solution)/shard_map/ppermute | solution.py:18
  15.0 14.7 %collective-permute-start.3 = (f32[512]{0:T(512)S(1)}, f32[512]{0:T(512)S(1)}, u32[]{:S(2)}, u32[]{:S(2)}) collective-permute-start(f32[512]{0:T(512)S(1)} %bitcast.395), channel_id=1, source_target_pairs={{0,31},{1,0},{2,1},{3,2},{4,3},{5,4},{6,5},{7,6},{8,7},{9,8},{10,9... | collective-permute-start | bytes 6152 | tf_op jit(solution)/shard_map/ppermute | solution.py:18
  15.0 20.0 %collective-permute-start.1 = (f32[512,256]{1,0:T(8,128)S(1)}, f32[512,256]{1,0:T(8,128)}, u32[]{:S(2)}, u32[]{:S(2)}) collective-permute-start(f32[512,256]{1,0:T(8,128)S(1)} %copy_bitcast_fusion), channel_id=1, source_target_pairs={{0,31},{1,0},{2,1},{3,2},{4,3},{5,4},{6,5},{7,6},{8,7},{9,8},{10,9... | collective-permute-start | bytes 1572872 | tf_op jit(solution)/shard_map/ppermute | solution.py:18
  36.1 1.2 copy-start.2
  64.9 87.3 %copy-start.7 = (f32[128]{0:T(128)}, f32[128]{0:T(128)S(1)}, u32[]{:S(2)}) copy-start(f32[128]{0:T(128)S(1)} %get-tuple-element.1422) | copy-start | bytes 1540
  96.6 55.6 %copy-start.8 = (f32[128]{0:T(128)}, f32[128]{0:T(128)S(1)}, u32[]{:S(2)}) copy-start(f32[128]{0:T(128)S(1)} %get-tuple-element.1423) | copy-start | bytes 1540
  122.8 0.5 copy-start.15
  122.8 29.4 %copy-start.9 = (f32[128]{0:T(128)}, f32[128]{0:T(128)S(1)}, u32[]{:S(2)}) copy-start(f32[128]{0:T(128)S(1)} %get-tuple-element.1424) | copy-start | bytes 1540
  151.6 0.6 copy-start.17
  151.6 26.8 %copy-start.10 = (f32[128]{0:T(128)}, f32[128]{0:T(128)S(1)}, u32[]{:S(2)}) copy-start(f32[128]{0:T(128)S(1)} %get-tuple-element.1425) | copy-start | bytes 1540
  152.2 26.2 %copy-start.11 = (f32[512]{0:T(512)}, f32[512]{0:T(512)S(1)}, u32[]{:S(2)}) copy-start(f32[512]{0:T(512)S(1)} %broadcast_multiply_fusion.1) | copy-start | bytes 6148
  152.2 5.1 %collective-permute-start.6 = (f32[512]{0:T(512)S(1)}, f32[512]{0:T(512)S(1)}, u32[]{:S(2)}, u32[]{:S(2)}) collective-permute-start(f32[512]{0:T(512)S(1)} %broadcast_multiply_fusion.1), channel_id=1, source_target_pairs={{0,1},{1,2},{2,3},{3,4},{4,5},{5,6},{6,7},{7,8},{8,9},{9,10},{10,1... | collective-permute-start | bytes 6152 | tf_op jit(solution)/shard_map/ppermute | solution.py:18
  152.3 5.1 %collective-permute-start.7 = (f32[512]{0:T(512)S(1)}, f32[512]{0:T(512)S(1)}, u32[]{:S(2)}, u32[]{:S(2)}) collective-permute-start(f32[512]{0:T(512)S(1)} %broadcast_multiply_fusion.1), channel_id=1, source_target_pairs={{0,31},{1,0},{2,1},{3,2},{4,3},{5,4},{6,5},{7,6},{8,7},{9,8},{10,9... | collective-permute-start | bytes 6152 | tf_op jit(solution)/shard_map/ppermute | solution.py:18
  154.1 16.9 %collective-permute-start.4 = (f32[512,256]{1,0:T(8,128)S(1)}, f32[512,256]{1,0:T(8,128)S(1)}, u32[]{:S(2)}, u32[]{:S(2)}) collective-permute-start(f32[512,256]{1,0:T(8,128)S(1)} %broadcast_multiply_fusion), channel_id=1, source_target_pairs={{0,1},{1,2},{2,3},{3,4},{4,5},{5,6},{6,7},{7,8},{8,9},{9,10},{10,1... | collective-permute-start | bytes 1572872 | tf_op jit(solution)/shard_map/ppermute | solution.py:18
  154.2 23.0 %collective-permute-start.5 = (f32[512,256]{1,0:T(8,128)S(1)}, f32[512,256]{1,0:T(8,128)S(1)}, u32[]{:S(2)}, u32[]{:S(2)}) collective-permute-start(f32[512,256]{1,0:T(8,128)S(1)} %broadcast_multiply_fusion), channel_id=1, source_target_pairs={{0,31},{1,0},{2,1},{3,2},{4,3},{5,4},{6,5},{7,6},{8,7},{9,8},{10,9... | collective-permute-start | bytes 1572872 | tf_op jit(solution)/shard_map/ppermute | solution.py:18
  217.2 0.6 copy-start.19
  348.4 5.4 %copy-start.1 = (f32[128,256]{1,0:T(8,128)S(1)}, f32[128,256]{1,0:T(8,128)}, u32[]{:S(2)}) copy-start(f32[128,256]{1,0:T(8,128)} %get-tuple-element.1429) | copy-start | bytes 393220
  349.1 4.7 collective-permute-start.10
  349.2 4.6 collective-permute-start.11
  351.9 16.9 %collective-permute-start.8 = (f32[512,256]{1,0:T(8,128)S(1)}, f32[512,256]{1,0:T(8,128)S(1)}, u32[]{:S(2)}, u32[]{:S(2)}) collective-permute-start(f32[512,256]{1,0:T(8,128)S(1)} %fusion.121), channel_id=1, source_target_pairs={{0,1},{1,2},{2,3},{3,4},{4,5},{5,6},{6,7},{7,8},{8,9},{9,10},{10,1... | collective-permute-start | bytes 1572872 | tf_op jit(solution)/shard_map/ppermute | solution.py:18
  352.0 23.0 %collective-permute-start.9 = (f32[512,256]{1,0:T(8,128)S(1)}, f32[512,256]{1,0:T(8,128)S(1)}, u32[]{:S(2)}, u32[]{:S(2)}) collective-permute-start(f32[512,256]{1,0:T(8,128)S(1)} %fusion.121), channel_id=1, source_target_pairs={{0,31},{1,0},{2,1},{3,2},{4,3},{5,4},{6,5},{7,6},{8,7},{9,8},{10,9... | collective-permute-start | bytes 1572872 | tf_op jit(solution)/shard_map/ppermute | solution.py:18
  376.3 32.3 %copy-start.20 = (s32[8]{0:T(128)S(1)}, s32[8]{0:T(128)}, u32[]{:S(2)}) copy-start(s32[8]{0:T(128)} %copy-done.19) | copy-start | bytes 100
  408.6 28.4 %copy-start.18 = (s32[8]{0:T(128)S(1)}, s32[8]{0:T(128)}, u32[]{:S(2)}) copy-start(s32[8]{0:T(128)} %get-tuple-element.2953) | copy-start | bytes 100
  437.0 28.4 %copy-start.16 = (s32[8]{0:T(128)S(1)}, s32[8]{0:T(128)}, u32[]{:S(2)}) copy-start(s32[8]{0:T(128)} %get-tuple-element.2951) | copy-start | bytes 100
  465.3 27.3 %copy-start.3 = (f32[128,2,128]{2,0,1:T(8,128)S(1)}, f32[128,2,128]{2,0,1:T(8,128)}, u32[]{:S(2)}) copy-start(f32[128,2,128]{2,0,1:T(8,128)} %get-tuple-element.1672) | copy-start | bytes 393220
  465.4 27.3 %copy-start.4 = (f32[128,2,128]{2,0,1:T(8,128)S(1)}, f32[128,2,128]{2,0,1:T(8,128)}, u32[]{:S(2)}) copy-start(f32[128,2,128]{2,0,1:T(8,128)} %get-tuple-element.1673) | copy-start | bytes 393220
  465.4 27.3 %copy-start.5 = (f32[128,2,128]{2,0,1:T(8,128)S(1)}, f32[128,2,128]{2,0,1:T(8,128)}, u32[]{:S(2)}) copy-start(f32[128,2,128]{2,0,1:T(8,128)} %get-tuple-element.1670) | copy-start | bytes 393220
  465.4 27.3 %copy-start.6 = (f32[128,2,128]{2,0,1:T(8,128)S(1)}, f32[128,2,128]{2,0,1:T(8,128)}, u32[]{:S(2)}) copy-start(f32[128,2,128]{2,0,1:T(8,128)} %get-tuple-element.1671) | copy-start | bytes 393220
  492.7 4.5 copy-start.12
  493.7 8.9 %all-to-all-start.1 = ((f32[512,2,128]{2,0,1:T(8,128)}), f32[512,2,128]{2,0,1:T(8,128)S(1)}, u32[]{:S(2)}, u32[]{:S(2)}) async-start(f32[512,2,128]{2,0,1:T(8,128)} %fusion.123), calls=%async_computation.1 | async-start | bytes 1048576 | tf_op jit(solution)/shard_map/all_to_all | solution.py:98
where the time goes:
time: 499 us; the launch traced here: 503 us
  matrix products  181 us (36%)
  loops' own time  136 us (27%)
  local copies, waits for them, and re-layouts  92.8 us (19%)
  waiting for transfers between devices  68.1 us (14%)
  starting transfers between devices  18 us (4%)
  other arithmetic  5.99 us (1%)
    another operation x12, loops' own time, accumulate(): lax.fori_loop(0, finishes[row_index], add_block, initial)  136 us
    dot_general x96, matrix products, add_block(): jnp.dot(matrix, segment, precision=HIGHEST_PRECISION, preferred_element_t...  121 us
    dynamic_slice x96, local copies, waits for them, and re-layouts, add_block(): columns[slot_index] - base_block  80.1 us
    dot_general x96, matrix products, add_block(): jnp.dot(matrix, segment_check, precision=HIGHEST_PRECISION, preferred_ele...  59.8 us
    ppermute x12, waiting for transfers between devices, shifted_2(): return lax.ppermute(value, axis, pairs)  57.7 us
    ppermute x12, starting transfers between devices, shifted_2(): return lax.ppermute(value, axis, pairs)  11.1 us
  transfers between devices with their start and end apart: 14, of which 8 were waited for; matrix products, arithmetic and copies ran while one was open for 2% of the time, Pallas kernels for 0%

commit v1 on v0

--- a/solution.py
+++ b/solution.py
@@ -1,15 +1,22 @@
+import functools
+
 import jax
 import jax.numpy as jnp
 from jax import lax
+from jax.experimental import pallas as pl
+from jax.experimental.pallas import tpu as pltpu
 from jax.sharding import PartitionSpec as P
 
 REACH = 4
+RIGHT_REACH = 3
+LIGHT = 3
 ITERS = 3
 
 
 CENTRE = 0.25
 HALF_WIDTH = 1.5
 HIGHEST_PRECISION = lax.Precision.HIGHEST
+MESH = pl.DeviceIdType.MESH
 
 
 def shifted_2(value, axis, steps):
@@ -68,7 +75,7 @@
     return (jnp.concatenate(pieces, 0), jnp.concatenate(piece_checks, 0))
 
 
-def per_device(start_vectors, ham_blocks, block_cols, block_counts, check_weights):
+def rows_split(start_vectors, ham_blocks, block_cols, block_counts, check_weights):
     row_vectors = lax.all_to_all(start_vectors, "col", split_axis=0, concat_axis=1, tiled=True)
     checks = jnp.dot(
         row_vectors, check_weights, precision=HIGHEST_PRECISION, preferred_element_type=jnp.float32
@@ -99,6 +106,283 @@
     return (filtered, current_check)
 
 
+def split2(x):
+    high = x.astype(jnp.bfloat16)
+    low = (x - high.astype(jnp.float32)).astype(jnp.bfloat16)
+    return high, low
+
+
+def beyond(count, slot):
+    return jnp.minimum(jnp.maximum(count - slot, 0), 1)
+
+
+def filter_kernel(
+    rows_n, v_ref, h_ref, tab_ref, tabh_ref, w_ref, out_ref, chk_ref,
+    hv, hr, es, em, er, tabv, tabp, a_ref, ea_ref, win, p_ref, y1, y2, halo, cs_s, cs_r,
+    send, recv, loc,
+):
+    r = lax.axis_index("row")
+    y = lax.axis_index("col")
+    right, left = lax.rem(r + 1, rows_n), lax.rem(r + rows_n - 1, rows_n)
+    core = lax.rem(r, 2)
+    sib = r + 1 - 2 * core
+    blocks, cap, size, _ = hv.shape
+    group = 2 * blocks
+    total = rows_n * group
+    heavy_slots = cap - LIGHT
+    half_rows = blocks // 2
+
+    barrier = pltpu.get_barrier_semaphore()
+    for target in ({"row": left}, {"row": right}, {"col": 1 - y}):
+        pl.semaphore_signal(barrier, inc=1, device_id=target, device_id_type=MESH)
+
+    own_copy = pltpu.make_async_copy(h_ref, hv, loc.at[0])
+    own_copy.start()
+    pl.semaphore_wait(barrier, 3)
+
+    def remote(src, dst, index, target):
+        return pltpu.make_async_remote_copy(
+            src_ref=src, dst_ref=dst, send_sem=send.at[index], recv_sem=recv.at[index],
+            device_id=target, device_id_type=MESH,
+        )
+
+    peer = {"col": 1 - y}
+    sibling = {"row": sib}
+    tab_copy = remote(tabh_ref, tabv, 0, peer)
+    light_copy = remote(h_ref.at[:, pl.ds(0, LIGHT)], hr, 1, peer)
+    merge_copy = remote(
+        h_ref.at[pl.ds(half_rows * (1 - core), half_rows), pl.ds(LIGHT, heavy_slots)], es, 2, sibling
+    )
+    mine = pl.ds(half_rows * core, half_rows)
+    cross_copy = remote(em, er.at[mine], 3, peer)
+    share_copy = remote(er.at[mine], er.at[mine], 4, sibling)
+    check_copy = remote(cs_s, cs_r, 5, peer)
+
+    def halo_copies(source, step):
+        own_rows = group * size
+        to_right = remote(
+            source.at[pl.ds(own_rows - REACH * size, REACH * size)],
+            halo.at[step, pl.ds(0, REACH * size)], 6 + 2 * step, {"row": right},
+        )
+        to_left = remote(
+            source.at[pl.ds(0, RIGHT_REACH * size)],
+            halo.at[step, pl.ds(REACH * size, RIGHT_REACH * size)], 7 + 2 * step, {"row": left},
+        )
+        return to_right, to_left
+
+    tab_copy.start()
+    merge_copy.start()
+    light_copy.start()
+    first = halo_copies(v_ref, 0)
+    first[0].start()
+    first[1].start()
+
+    def put_window(source, src_at, dst_at, count):
+        def one(i, _):
+            at = pl.multiple_of(src_at + i * size, size)
+            high, low = split2(source[pl.ds(at, size), :])
+            win[dst_at + i, :, pl.ds(0, size)] = high
+            win[dst_at + i, :, pl.ds(size, size)] = low
+            return 0
+
+        lax.fori_loop(0, count, one, 0)
+
+    def put_halo(step):
+        put_window(halo.at[step], 0, 0, REACH)
+        put_window(halo.at[step], REACH * size, REACH + group, RIGHT_REACH)
+
+    def scalar(i, j):
+        return tab_ref[i, j], tabp[i, j]
+
+    own_is_heavy = beyond(tab_ref[0, cap], LIGHT)
+    own_heavy = own_is_heavy.astype(jnp.float32)
+
+    own_copy.wait()
+    merge_copy.wait_recv()
+
+    def merge(i, _):
+        a = hv[half_rows * core + i, pl.ds(LIGHT, heavy_slots)]
+        em[i] = a * own_heavy + es[i] * (1.0 - own_heavy)
+        return 0
+
+    lax.fori_loop(0, half_rows, merge, 0)
+    cross_copy.start()
+
+    def put_light(source, table, half):
+        def one(i, _):
+            count = table[i, cap]
+            for j in range(LIGHT):
+                live = beyond(count, j).astype(jnp.float32)
+                high, low = split2(source[i, j] * live)
+                a_ref[half * blocks + i, pl.ds(0, size), pl.ds(j * size, size)] = high
+                a_ref[half * blocks + i, pl.ds(size, size), pl.ds(j * size, size)] = low
+            return 0
+
+        lax.fori_loop(0, blocks, one, 0)
+
+    put_light(hv, tab_ref, y)
+    put_window(v_ref, 0, REACH, group)
+
+    tab_copy.wait_recv()
+    tab_local = pltpu.make_async_copy(tabv, tabp, loc.at[1])
+    tab_local.start()
+    tab_local.wait()
+    peer_heavy = beyond(tabp[0, cap], LIGHT).astype(jnp.float32)
+
+    first[0].wait_recv()
+    first[1].wait_recv()
+    put_halo(0)
+
+    light_copy.wait_recv()
+    put_light(hr, tabp, 1 - y)
+
+    cross_copy.wait_recv()
+    share_copy.start()
+    share_copy.wait_recv()
+
+    def put_heavy(i, _):
+        own_count, peer_count = scalar(i, cap)
+        for j in range(heavy_slots):
+            own_live = beyond(own_count, LIGHT + j).astype(jnp.float32)
+            peer_live = beyond(peer_count, LIGHT + j).astype(jnp.float32) * (1.0 - own_heavy)
+            high, low = split2(hv[i, LIGHT + j] * own_live + er[i, j] * peer_live)
+            ea_ref[i, pl.ds(0, size), pl.ds(j * size, size)] = high
+            ea_ref[i, pl.ds(size, size), pl.ds(j * size, size)] = low
+        return 0
+
+    lax.fori_loop(0, blocks, put_heavy, 0)
+
+    base = r * group - REACH + total
+
+    def tile(col):
+        return win[jnp.minimum(lax.rem(col - base + 2 * total, total), win.shape[0] - 1)]
+
+    def product(matrix, cols):
+        tiles = jnp.concatenate([tile(col) for col in cols], 0)
+        full = jnp.dot(matrix, tiles, preferred_element_type=jnp.float32)
+        big = full[:size, :size]
+        small = full[:size, size:] + full[size:, :size] + full[size:, size:]
+        return big + small
+
+    def heavy_products():
+        def one(i, _):
+            cols = []
+            for j in range(heavy_slots):
+                own_col, peer_col = scalar(i, LIGHT + j)
+                cols.append(peer_col + own_is_heavy * (own_col - peer_col))
+            p_ref[i] = product(ea_ref[i], cols)
+            return 0
+
+        lax.fori_loop(0, blocks, one, 0)
+
+    def rows(half, source, older, target):
+        mine = y * half + (1 - y) * (1 - half)
+        share = mine.astype(jnp.float32)
+        flag = own_heavy * share + peer_heavy * (1.0 - share)
+
+        def one(i, _):
+            cols = []
+            for j in range(LIGHT):
+                own_col, peer_col = scalar(i, j)
+                cols.append(peer_col + mine * (own_col - peer_col))
+            image = product(a_ref[half * blocks + i], cols) + p_ref[i] * flag
+            at = pl.ds(pl.multiple_of((half * blocks + i) * size, size), size)
+            value = (image - CENTRE * source[at, :]) * (1.0 / HALF_WIDTH)
+            if older is not None:
+                value = 2.0 * value - older[at, :]
+            target[at, :] = value
+            return 0
+
+        lax.fori_loop(0, blocks, one, 0)
+
+    chain = ((v_ref, None, y1), (y1, v_ref, y2), (y2, y1, out_ref))
+    started = [*first]
+    for step in range(ITERS):
+        source, older, target = chain[step]
+        if step:
+            put_window(source, 0, REACH, group)
+            started[2 * step].wait_recv()
+            started[2 * step + 1].wait_recv()
+            put_halo(step)
+        heavy_products()
+        if step < ITERS - 1:
+            following = halo_copies(target, step + 1)
+            started += following
+            rows(1, source, older, target)
+            following[0].start()
+            rows(0, source, older, target)
+            following[1].start()
+        else:
+            rows(1, source, older, target)
+            rows(0, source, older, target)
+
+    weights = jnp.where(y == 0, w_ref[:, :size], w_ref[:, size:])
+
+    def partial(half):
+        at = pl.ds(pl.multiple_of(half * blocks * size, size), blocks * size)
+        return lax.dot_general(
+            weights, out_ref[at, :], (((1,), (1,)), ((), ())),
+            precision=HIGHEST_PRECISION, preferred_element_type=jnp.float32,
+        )
+
+    cs_s[...] = partial(1 - y)
+    check_copy.start()
+    own_part = partial(y)
+    check_copy.wait_recv()
+    chk_ref[...] = own_part + cs_r[...]
+
+    for copy in (tab_copy, light_copy, merge_copy, cross_copy, share_copy, check_copy, *started):
+        copy.wait_send()
+
+
+def columns_split(start_vectors, ham_blocks, block_cols, block_counts, check_weights):
+    blocks, cap, size, _ = ham_blocks.shape
+    rows_n = lax.axis_size("row")
+    group = 2 * blocks
+    height, width = start_vectors.shape
+    table = jnp.concatenate([block_cols, block_counts[:, None]], 1)
+    table = jnp.pad(table, ((0, 8 - blocks), (0, 128 - cap - 1)))
+    window = REACH + group + RIGHT_REACH
+    f32, bf16 = jnp.float32, jnp.bfloat16
+    heavy = cap - LIGHT
+    vmem = pl.BlockSpec(memory_space=pltpu.VMEM)
+    anywhere = pl.BlockSpec(memory_space=pl.ANY)
+    filtered, check = pl.pallas_call(
+        functools.partial(filter_kernel, rows_n),
+        out_shape=(
+            jax.ShapeDtypeStruct((height, width), f32),
+            jax.ShapeDtypeStruct((1, blocks * size), f32),
+        ),
+        in_specs=[vmem, anywhere, pl.BlockSpec(memory_space=pltpu.SMEM), anywhere, vmem],
+        out_specs=(vmem, vmem),
+        scratch_shapes=[
+            pltpu.VMEM((blocks, cap, size, size), f32),
+            pltpu.VMEM((blocks, LIGHT, size, size), f32),
+            pltpu.VMEM((blocks // 2, heavy, size, size), f32),
+            pltpu.VMEM((blocks // 2, heavy, size, size), f32),
+            pltpu.VMEM((blocks, heavy, size, size), f32),
+            pltpu.VMEM((8, 128), jnp.int32),
+            pltpu.SMEM((8, 128), jnp.int32),
+            pltpu.VMEM((group, 2 * size, LIGHT * size), bf16),
+            pltpu.VMEM((blocks, 2 * size, heavy * size), bf16),
+            pltpu.VMEM((window, size, 2 * width), bf16),
+            pltpu.VMEM((blocks, size, width), f32),
+            pltpu.VMEM((height, width), f32),
+            pltpu.VMEM((height, width), f32),
+            pltpu.VMEM((ITERS, (REACH + RIGHT_REACH) * size, width), f32),
+            pltpu.VMEM((1, blocks * size), f32),
+            pltpu.VMEM((1, blocks * size), f32),
+            pltpu.SemaphoreType.DMA((6 + 2 * ITERS,)),
+            pltpu.SemaphoreType.DMA((6 + 2 * ITERS,)),
+            pltpu.SemaphoreType.DMA((2,)),
+        ],
+        compiler_params=pltpu.CompilerParams(
+            collective_id=0, has_side_effects=True, vmem_limit_bytes=40 * 1024 * 1024
+        ),
+    )(start_vectors, ham_blocks, table, table, check_weights.reshape(1, -1))
+    return (filtered, check.reshape(-1))
+
+
 def solution(mesh):
     placed = (
         P("row", "col"),
@@ -107,8 +391,10 @@
         P(("row", "col")),
         P(),
     )
+    devices = mesh.shape["row"] * mesh.shape["col"]
+    one_heavy = devices < 64 and mesh.shape["col"] == 2 and mesh.shape["row"] >= 4 and mesh.shape["row"] % 2 == 0
     return jax.shard_map(
-        per_device,
+        columns_split if one_heavy else rows_split,
         mesh=mesh,
         in_specs=placed,
         out_specs=(P("row", "col"), P(("row", "col"))),

time: 499 us -> 69.6 us (0.14)
  the two profiles are of different devices: /device:TPU:27 before, /device:TPU:2 now
where the time goes in v1:
time: 69.6 us; the launch traced here: 69.4 us
  Pallas kernels  62.6 us (90%)
  local copies, waits for them, and re-layouts  5.43 us (8%)
  other arithmetic  0.75 us (1%)
    pallas_call x1, Pallas kernels, columns_split(): pl.pallas_call(functools.partial(filter_kernel, rows_n), out_shape=(jax.S...  62.6 us
    unnamed x8, local copies, waits for them, and re-layouts  4.68 us

profile of v1, /device:TPU:2, one launch (start us, length us, event | category | flops | bytes accessed | tf_op | source)
XLA Modules:
  0.0 69.4 jit_solution(17525949049735004872)
XLA Ops:
  0.6 0.7 %copy.7 = s32[4,1]{1,0:T(4,128)S(1)} copy(s32[4,1]{0,1:T(1,128)} %bitcast.5) | data formatting | bytes 32 | tf_op jit(solution)/shard_map/broadcast_in_dim | solution.py:343
  1.4 0.8 %pad_add_fusion = s32[4,9]{1,0:T(4,128)S(1)} fusion(s32[4,1]{1,0:T(4,128)S(1)} %copy.7, s32[4,8]{1,0:T(4,128)} %param.7), kind=kLoop, calls=%fused_computation | loop fusion | flops 36 | bytes 288 | tf_op jit(solution)/shard_map/concatenate | solution.py:343
  2.1 0.0 copy-start
  2.1 1.6 %copy-done = f32[4,8,128,128]{3,2,1,0:T(8,128)S(1)} copy-done((f32[4,8,128,128]{3,2,1,0:T(8,128)S(1)}, f32[4,8,128,128]{3,2,1,0:T(8,128)}, u32[]{:S(2)}) %copy-start) | copy-done | bytes 2097176
  3.7 0.0 copy-start.1
  3.7 1.0 %copy-done.1 = f32[1024,128]{1,0:T(8,128)S(1)} copy-done((f32[1024,128]{1,0:T(8,128)S(1)}, f32[1024,128]{1,0:T(8,128)}, u32[]{:S(2)}) %copy-start.1) | copy-done | bytes 524312
  4.8 0.0 copy-start.2
  4.8 0.7 copy-done.2
  5.4 62.6 %shard_map.68 = (f32[1024,128]{1,0:T(8,128)S(1)}, f32[1,512]{1,0:T(1,128)S(1)}) custom-call(f32[1024,128]{1,0:T(8,128)S(1)} %copy-done.1, f32[4,8,128,128]{3,2,1,0:T(8,128)S(1)} %copy-done, s32[8,128]{1,0:T(8,128)S(1)} %pad.4.tab_ref.tabh_ref, s32[8,128]{1,0:T(8,128)S(1)} %pad.4.tab_ref.tabh_ref, f32[1,256]{1,0:T(1,128)S(1)} %bitcast.4), custom_call_target="tpu_custom_call" | custom-call | tf_op jit(solution)/shard_map/pallas_call | solution.py:350
  68.0 0.8 %copy.10 = f32[1024,128]{1,0:T(8,128)} copy(f32[1024,128]{1,0:T(8,128)S(1)} %get-tuple-element.8) | data formatting | bytes 1048576
  68.8 0.6 copy.11
  (1 shorter events, 0.0 us)
Async XLA Ops:
  2.1 1.6 %copy-start = (f32[4,8,128,128]{3,2,1,0:T(8,128)S(1)}, f32[4,8,128,128]{3,2,1,0:T(8,128)}, u32[]{:S(2)}) copy-start(f32[4,8,128,128]{3,2,1,0:T(8,128)} %h_ref.1) | copy-start | bytes 6291460
  3.7 1.0 %copy-start.1 = (f32[1024,128]{1,0:T(8,128)S(1)}, f32[1024,128]{1,0:T(8,128)}, u32[]{:S(2)}) copy-start(f32[1024,128]{1,0:T(8,128)} %v_ref.1) | copy-start | bytes 1572868
  4.8 0.7 copy-start.2

commit v2 on v1

--- a/solution.py
+++ b/solution.py
@@ -117,8 +117,8 @@
 
 
 def filter_kernel(
-    rows_n, v_ref, h_ref, tab_ref, tabh_ref, w_ref, out_ref, chk_ref,
-    hv, hr, es, em, er, tabv, tabp, a_ref, ea_ref, win, p_ref, y1, y2, halo, cs_s, cs_r,
+    rows_n, v_hbm, h_ref, cols_ref, counts_ref, colsh_ref, countsh_ref, w_hbm, out_ref, chk_ref,
+    v_ref, w_ref, hv, hr, es, em, er, colsp, countsp, a_ref, ea_ref, win, p_ref, y1, y2, halo, cs_s, cs_r,
     send, recv, loc,
 ):
     r = lax.axis_index("row")
@@ -137,7 +137,11 @@
         pl.semaphore_signal(barrier, inc=1, device_id=target, device_id_type=MESH)
 
     own_copy = pltpu.make_async_copy(h_ref, hv, loc.at[0])
+    vector_copy = pltpu.make_async_copy(v_hbm, v_ref, loc.at[1])
+    weight_copy = pltpu.make_async_copy(w_hbm, w_ref, loc.at[2])
     own_copy.start()
+    vector_copy.start()
+    weight_copy.start()
     pl.semaphore_wait(barrier, 3)
 
     def remote(src, dst, index, target):
@@ -148,7 +152,8 @@
 
     peer = {"col": 1 - y}
     sibling = {"row": sib}
-    tab_copy = remote(tabh_ref, tabv, 0, peer)
+    cols_copy = remote(colsh_ref, colsp, 0, peer)
+    counts_copy = remote(countsh_ref, countsp, 6 + 2 * ITERS, peer)
     light_copy = remote(h_ref.at[:, pl.ds(0, LIGHT)], hr, 1, peer)
     merge_copy = remote(
         h_ref.at[pl.ds(half_rows * (1 - core), half_rows), pl.ds(LIGHT, heavy_slots)], es, 2, sibling
@@ -170,10 +175,11 @@
         )
         return to_right, to_left
 
-    tab_copy.start()
+    cols_copy.start()
+    counts_copy.start()
     merge_copy.start()
     light_copy.start()
-    first = halo_copies(v_ref, 0)
+    first = halo_copies(v_hbm, 0)
     first[0].start()
     first[1].start()
 
@@ -185,16 +191,16 @@
             win[dst_at + i, :, pl.ds(size, size)] = low
             return 0
 
-        lax.fori_loop(0, count, one, 0)
+        lax.fori_loop(0, count, one, 0, unroll=True)
 
     def put_halo(step):
         put_window(halo.at[step], 0, 0, REACH)
         put_window(halo.at[step], REACH * size, REACH + group, RIGHT_REACH)
 
     def scalar(i, j):
-        return tab_ref[i, j], tabp[i, j]
-
-    own_is_heavy = beyond(tab_ref[0, cap], LIGHT)
+        return cols_ref[i, j], colsp[i, j]
+
+    own_is_heavy = beyond(counts_ref[0, 0], LIGHT)
     own_heavy = own_is_heavy.astype(jnp.float32)
 
     own_copy.wait()
@@ -205,12 +211,12 @@
         em[i] = a * own_heavy + es[i] * (1.0 - own_heavy)
         return 0
 
-    lax.fori_loop(0, half_rows, merge, 0)
+    lax.fori_loop(0, half_rows, merge, 0, unroll=True)
     cross_copy.start()
 
     def put_light(source, table, half):
         def one(i, _):
-            count = table[i, cap]
+            count = table[0, i]
             for j in range(LIGHT):
                 live = beyond(count, j).astype(jnp.float32)
                 high, low = split2(source[i, j] * live)
@@ -218,30 +224,29 @@
                 a_ref[half * blocks + i, pl.ds(size, size), pl.ds(j * size, size)] = low
             return 0
 
-        lax.fori_loop(0, blocks, one, 0)
-
-    put_light(hv, tab_ref, y)
+        lax.fori_loop(0, blocks, one, 0, unroll=True)
+
+    vector_copy.wait()
+    put_light(hv, counts_ref, y)
     put_window(v_ref, 0, REACH, group)
 
-    tab_copy.wait_recv()
-    tab_local = pltpu.make_async_copy(tabv, tabp, loc.at[1])
-    tab_local.start()
-    tab_local.wait()
-    peer_heavy = beyond(tabp[0, cap], LIGHT).astype(jnp.float32)
+    cols_copy.wait_recv()
+    counts_copy.wait_recv()
+    peer_heavy = beyond(countsp[0, 0], LIGHT).astype(jnp.float32)
 
     first[0].wait_recv()
     first[1].wait_recv()
     put_halo(0)
 
     light_copy.wait_recv()
-    put_light(hr, tabp, 1 - y)
+    put_light(hr, countsp, 1 - y)
 
     cross_copy.wait_recv()
     share_copy.start()
     share_copy.wait_recv()
 
     def put_heavy(i, _):
-        own_count, peer_count = scalar(i, cap)
+        own_count, peer_count = counts_ref[0, i], countsp[0, i]
         for j in range(heavy_slots):
             own_live = beyond(own_count, LIGHT + j).astype(jnp.float32)
             peer_live = beyond(peer_count, LIGHT + j).astype(jnp.float32) * (1.0 - own_heavy)
@@ -250,7 +255,7 @@
             ea_ref[i, pl.ds(size, size), pl.ds(j * size, size)] = low
         return 0
 
-    lax.fori_loop(0, blocks, put_heavy, 0)
+    lax.fori_loop(0, blocks, put_heavy, 0, unroll=True)
 
     base = r * group - REACH + total
 
@@ -273,7 +278,7 @@
             p_ref[i] = product(ea_ref[i], cols)
             return 0
 
-        lax.fori_loop(0, blocks, one, 0)
+        lax.fori_loop(0, blocks, one, 0, unroll=True)
 
     def rows(half, source, older, target):
         mine = y * half + (1 - y) * (1 - half)
@@ -293,7 +298,7 @@
             target[at, :] = value
             return 0
 
-        lax.fori_loop(0, blocks, one, 0)
+        lax.fori_loop(0, blocks, one, 0, unroll=True)
 
     chain = ((v_ref, None, y1), (y1, v_ref, y2), (y2, y1, out_ref))
     started = [*first]
@@ -316,14 +321,20 @@
             rows(1, source, older, target)
             rows(0, source, older, target)
 
+    weight_copy.wait()
     weights = jnp.where(y == 0, w_ref[:, :size], w_ref[:, size:])
+    w_high, w_rest = split2(weights)
+    w_low = (weights - w_high.astype(jnp.float32) - w_rest.astype(jnp.float32)).astype(jnp.bfloat16)
+    w_parts = jnp.concatenate([w_high, w_rest, w_low, jnp.zeros((13, size), jnp.bfloat16)], 0)
 
     def partial(half):
         at = pl.ds(pl.multiple_of(half * blocks * size, size), blocks * size)
-        return lax.dot_general(
-            weights, out_ref[at, :], (((1,), (1,)), ((), ())),
-            precision=HIGHEST_PRECISION, preferred_element_type=jnp.float32,
-        )
+        total_dot = 0.0
+        for part in split2(out_ref[at, :]):
+            total_dot += lax.dot_general(
+                w_parts, part, (((1,), (1,)), ((), ())), preferred_element_type=jnp.float32
+            )
+        return jnp.sum(total_dot, 0, keepdims=True)
 
     cs_s[...] = partial(1 - y)
     check_copy.start()
@@ -331,7 +342,7 @@
     check_copy.wait_recv()
     chk_ref[...] = own_part + cs_r[...]
 
-    for copy in (tab_copy, light_copy, merge_copy, cross_copy, share_copy, check_copy, *started):
+    for copy in (cols_copy, counts_copy, light_copy, merge_copy, cross_copy, share_copy, check_copy, *started):
         copy.wait_send()
 
 
@@ -340,12 +351,12 @@
     rows_n = lax.axis_size("row")
     group = 2 * blocks
     height, width = start_vectors.shape
-    table = jnp.concatenate([block_cols, block_counts[:, None]], 1)
-    table = jnp.pad(table, ((0, 8 - blocks), (0, 128 - cap - 1)))
+    counts = block_counts.reshape(1, blocks)
     window = REACH + group + RIGHT_REACH
     f32, bf16 = jnp.float32, jnp.bfloat16
     heavy = cap - LIGHT
     vmem = pl.BlockSpec(memory_space=pltpu.VMEM)
+    smem = pl.BlockSpec(memory_space=pltpu.SMEM)
     anywhere = pl.BlockSpec(memory_space=pl.ANY)
     filtered, check = pl.pallas_call(
         functools.partial(filter_kernel, rows_n),
@@ -353,16 +364,18 @@
             jax.ShapeDtypeStruct((height, width), f32),
             jax.ShapeDtypeStruct((1, blocks * size), f32),
         ),
-        in_specs=[vmem, anywhere, pl.BlockSpec(memory_space=pltpu.SMEM), anywhere, vmem],
+        in_specs=[anywhere, anywhere, smem, smem, anywhere, anywhere, anywhere],
         out_specs=(vmem, vmem),
         scratch_shapes=[
+            pltpu.VMEM((height, width), f32),
+            pltpu.VMEM((1, 2 * width), f32),
             pltpu.VMEM((blocks, cap, size, size), f32),
             pltpu.VMEM((blocks, LIGHT, size, size), f32),
             pltpu.VMEM((blocks // 2, heavy, size, size), f32),
             pltpu.VMEM((blocks // 2, heavy, size, size), f32),
             pltpu.VMEM((blocks, heavy, size, size), f32),
-            pltpu.VMEM((8, 128), jnp.int32),
-            pltpu.SMEM((8, 128), jnp.int32),
+            pltpu.SMEM((blocks, cap), jnp.int32),
+            pltpu.SMEM((1, blocks), jnp.int32),
             pltpu.VMEM((group, 2 * size, LIGHT * size), bf16),
             pltpu.VMEM((blocks, 2 * size, heavy * size), bf16),
             pltpu.VMEM((window, size, 2 * width), bf16),
@@ -372,14 +385,14 @@
             pltpu.VMEM((ITERS, (REACH + RIGHT_REACH) * size, width), f32),
             pltpu.VMEM((1, blocks * size), f32),
             pltpu.VMEM((1, blocks * size), f32),
-            pltpu.SemaphoreType.DMA((6 + 2 * ITERS,)),
-            pltpu.SemaphoreType.DMA((6 + 2 * ITERS,)),
-            pltpu.SemaphoreType.DMA((2,)),
+            pltpu.SemaphoreType.DMA((7 + 2 * ITERS,)),
+            pltpu.SemaphoreType.DMA((7 + 2 * ITERS,)),
+            pltpu.SemaphoreType.DMA((3,)),
         ],
         compiler_params=pltpu.CompilerParams(
-            collective_id=0, has_side_effects=True, vmem_limit_bytes=40 * 1024 * 1024
+            collective_id=0, has_side_effects=True, vmem_limit_bytes=60 * 1024 * 1024
         ),
-    )(start_vectors, ham_blocks, table, table, check_weights.reshape(1, -1))
+    )(start_vectors, ham_blocks, block_cols, counts, block_cols, counts, check_weights.reshape(1, -1))
     return (filtered, check.reshape(-1))
 
 

time: 69.6 us -> 61.7 us (0.89)
  the two profiles are of different devices: /device:TPU:2 before, /device:TPU:10 now
where the time goes in v2:
time: 61.7 us; the launch traced here: 61.5 us
  Pallas kernels  57.7 us (94%)
  local copies, waits for them, and re-layouts  3.12 us (5%)
  between operations  0.64 us (1%)
    pallas_call x1, Pallas kernels, columns_split(): pl.pallas_call(functools.partial(filter_kernel, rows_n), out_shape=(jax.S...  57.7 us
    unnamed x2, local copies, waits for them, and re-layouts  3.12 us

profile of v2, /device:TPU:10, one launch (start us, length us, event | category | flops | bytes accessed | tf_op | source)
XLA Modules:
  0.0 61.5 jit_solution(2793437852251313704)
XLA Ops:
  0.6 57.7 %shard_map.68 = (f32[1024,128]{1,0:T(8,128)}, f32[1,512]{1,0:T(1,128)}) custom-call(f32[1024,128]{1,0:T(8,128)} %v_hbm.1, f32[4,8,128,128]{3,2,1,0:T(8,128)} %h_ref.1, s32[4,8]{1,0:T(4,128)} %colsh_ref.1, s32[1,4]{1,0:T(1,128)} %bitcast.3, s32[4,8]{1,0:T(4,128)} %colsh_ref.1, s32[1,4]{1,0:T(1,128)} %bitcast.4, f32[1,256]{1,0:T(1,128)} %bitcast.6), custom_call_target="tpu_custom_call" | custom-call | tf_op jit(solution)/shard_map/pallas_call | solution.py:361
  58.3 1.9 %copy.9 = f32[1024,128]{1,0:T(8,128)} copy(f32[1024,128]{1,0:T(8,128)} %get-tuple-element.8) | data formatting | bytes 1048576
  60.2 1.3 %copy.10 = f32[512]{0:T(512)} copy(f32[512]{0:T(512)} %bitcast.5) | data formatting | bytes 4096

commit v3 on v2

--- a/solution.py
+++ b/solution.py
@@ -118,22 +118,25 @@
 
 def filter_kernel(
     rows_n, v_hbm, h_ref, cols_ref, counts_ref, colsh_ref, countsh_ref, w_hbm, out_ref, chk_ref,
-    v_ref, w_ref, hv, hr, es, em, er, colsp, countsp, a_ref, ea_ref, win, p_ref, y1, y2, halo, cs_s, cs_r,
-    send, recv, loc,
+    v_ref, w_ref, hv, hr, st, es, em, ex, ec, er, colsp, countsp, a_ref, ea_ref, win, p_ref, y1, y2,
+    halo, cs_s, cs_r, send, recv, loc,
 ):
     r = lax.axis_index("row")
     y = lax.axis_index("col")
     right, left = lax.rem(r + 1, rows_n), lax.rem(r + rows_n - 1, rows_n)
     core = lax.rem(r, 2)
-    sib = r + 1 - 2 * core
+    pair = lax.rem(r // 2, 2)
     blocks, cap, size, _ = hv.shape
     group = 2 * blocks
     total = rows_n * group
     heavy_slots = cap - LIGHT
     half_rows = blocks // 2
+    peer = {"col": 1 - y}
+    sibling = {"row": r + 1 - 2 * core}
+    across = {"row": r + 2 - 4 * pair}
 
     barrier = pltpu.get_barrier_semaphore()
-    for target in ({"row": left}, {"row": right}, {"col": 1 - y}):
+    for target in ({"row": left}, {"row": right}, across, peer):
         pl.semaphore_signal(barrier, inc=1, device_id=target, device_id_type=MESH)
 
     own_copy = pltpu.make_async_copy(h_ref, hv, loc.at[0])
@@ -142,7 +145,7 @@
     own_copy.start()
     vector_copy.start()
     weight_copy.start()
-    pl.semaphore_wait(barrier, 3)
+    pl.semaphore_wait(barrier, 4)
 
     def remote(src, dst, index, target):
         return pltpu.make_async_remote_copy(
@@ -150,112 +153,121 @@
             device_id=target, device_id_type=MESH,
         )
 
-    peer = {"col": 1 - y}
-    sibling = {"row": sib}
+    mine_row = half_rows * core + pair
+    other_row = half_rows * core + 1 - pair
     cols_copy = remote(colsh_ref, colsp, 0, peer)
-    counts_copy = remote(countsh_ref, countsp, 6 + 2 * ITERS, peer)
-    light_copy = remote(h_ref.at[:, pl.ds(0, LIGHT)], hr, 1, peer)
-    merge_copy = remote(
-        h_ref.at[pl.ds(half_rows * (1 - core), half_rows), pl.ds(LIGHT, heavy_slots)], es, 2, sibling
-    )
-    mine = pl.ds(half_rows * core, half_rows)
-    cross_copy = remote(em, er.at[mine], 3, peer)
-    share_copy = remote(er.at[mine], er.at[mine], 4, sibling)
-    check_copy = remote(cs_s, cs_r, 5, peer)
+    counts_copy = remote(countsh_ref, countsp, 1, peer)
+
+    def light_part(part):
+        at = pl.ds(half_rows * part, half_rows)
+        return remote(h_ref.at[at, pl.ds(0, LIGHT)], hr.at[at], 2 + part, peer)
+
+    light_copies = (light_part(0), light_part(1))
+    chip_copy = remote(st, es, 4, sibling)
+    pair_copy = remote(em.at[1 - pair], ex, 5, across)
+    cross_copy = remote(ec, er.at[mine_row], 6, peer)
+    pair_share = remote(er.at[mine_row], er.at[mine_row], 7, across)
+    chip_share = remote(er.at[mine_row], er.at[mine_row], 8, sibling)
+    chip_share_2 = remote(er.at[other_row], er.at[other_row], 9, sibling)
+    check_copy = remote(cs_s, cs_r, 10, peer)
 
     def halo_copies(source, step):
         own_rows = group * size
         to_right = remote(
             source.at[pl.ds(own_rows - REACH * size, REACH * size)],
-            halo.at[step, pl.ds(0, REACH * size)], 6 + 2 * step, {"row": right},
+            halo.at[step, pl.ds(0, REACH * size)], 11 + 2 * step, {"row": right},
         )
         to_left = remote(
             source.at[pl.ds(0, RIGHT_REACH * size)],
-            halo.at[step, pl.ds(REACH * size, RIGHT_REACH * size)], 7 + 2 * step, {"row": left},
+            halo.at[step, pl.ds(REACH * size, RIGHT_REACH * size)], 12 + 2 * step, {"row": left},
         )
         return to_right, to_left
 
     cols_copy.start()
     counts_copy.start()
-    merge_copy.start()
-    light_copy.start()
-    first = halo_copies(v_hbm, 0)
-    first[0].start()
-    first[1].start()
+    light_copies[0].start()
+
+    def loop(count, body):
+        def one(i, carry):
+            body(i)
+            return carry
+
+        lax.fori_loop(0, count, one, 0, unroll=True)
 
     def put_window(source, src_at, dst_at, count):
-        def one(i, _):
+        def one(i):
             at = pl.multiple_of(src_at + i * size, size)
             high, low = split2(source[pl.ds(at, size), :])
             win[dst_at + i, :, pl.ds(0, size)] = high
             win[dst_at + i, :, pl.ds(size, size)] = low
-            return 0
-
-        lax.fori_loop(0, count, one, 0, unroll=True)
+
+        loop(count, one)
 
     def put_halo(step):
         put_window(halo.at[step], 0, 0, REACH)
         put_window(halo.at[step], REACH * size, REACH + group, RIGHT_REACH)
 
-    def scalar(i, j):
-        return cols_ref[i, j], colsp[i, j]
-
     own_is_heavy = beyond(counts_ref[0, 0], LIGHT)
     own_heavy = own_is_heavy.astype(jnp.float32)
 
     own_copy.wait()
-    merge_copy.wait_recv()
-
-    def merge(i, _):
-        a = hv[half_rows * core + i, pl.ds(LIGHT, heavy_slots)]
-        em[i] = a * own_heavy + es[i] * (1.0 - own_heavy)
-        return 0
-
-    lax.fori_loop(0, half_rows, merge, 0, unroll=True)
-    cross_copy.start()
-
-    def put_light(source, table, half):
-        def one(i, _):
-            count = table[0, i]
+
+    def stage(i):
+        st[i] = hv[half_rows * (1 - core) + i, pl.ds(LIGHT, heavy_slots)] * own_heavy
+
+    loop(half_rows, stage)
+    chip_copy.start()
+
+    def put_light(source, table, half, first_row, count):
+        def one(i):
+            i = first_row + i
+            live_count = table[0, i]
             for j in range(LIGHT):
-                live = beyond(count, j).astype(jnp.float32)
+                live = beyond(live_count, j).astype(jnp.float32)
                 high, low = split2(source[i, j] * live)
                 a_ref[half * blocks + i, pl.ds(0, size), pl.ds(j * size, size)] = high
                 a_ref[half * blocks + i, pl.ds(size, size), pl.ds(j * size, size)] = low
-            return 0
-
-        lax.fori_loop(0, blocks, one, 0, unroll=True)
-
+
+        loop(count, one)
+
+    def put_heavy(with_peer):
+        def one(i):
+            for j in range(heavy_slots):
+                live = beyond(counts_ref[0, i], LIGHT + j).astype(jnp.float32)
+                value = hv[i, LIGHT + j] * live
+                if with_peer:
+                    live = beyond(countsp[0, i], LIGHT + j).astype(jnp.float32) * (1.0 - own_heavy)
+                    value = value + er[i, j] * live
+                high, low = split2(value)
+                ea_ref[i, pl.ds(0, size), pl.ds(j * size, size)] = high
+                ea_ref[i, pl.ds(size, size), pl.ds(j * size, size)] = low
+
+        loop(blocks, one)
+
+    put_light(hv, counts_ref, y, 0, blocks)
+    chip_copy.wait_recv()
+
+    def merge(i):
+        em[i] = hv[half_rows * core + i, pl.ds(LIGHT, heavy_slots)] * own_heavy + es[i]
+
+    loop(half_rows, merge)
+    pair_copy.start()
+
+    put_heavy(False)
     vector_copy.wait()
-    put_light(hv, counts_ref, y)
     put_window(v_ref, 0, REACH, group)
-
     cols_copy.wait_recv()
     counts_copy.wait_recv()
     peer_heavy = beyond(countsp[0, 0], LIGHT).astype(jnp.float32)
 
-    first[0].wait_recv()
-    first[1].wait_recv()
-    put_halo(0)
-
-    light_copy.wait_recv()
-    put_light(hr, countsp, 1 - y)
-
-    cross_copy.wait_recv()
-    share_copy.start()
-    share_copy.wait_recv()
-
-    def put_heavy(i, _):
-        own_count, peer_count = counts_ref[0, i], countsp[0, i]
-        for j in range(heavy_slots):
-            own_live = beyond(own_count, LIGHT + j).astype(jnp.float32)
-            peer_live = beyond(peer_count, LIGHT + j).astype(jnp.float32) * (1.0 - own_heavy)
-            high, low = split2(hv[i, LIGHT + j] * own_live + er[i, j] * peer_live)
-            ea_ref[i, pl.ds(0, size), pl.ds(j * size, size)] = high
-            ea_ref[i, pl.ds(size, size), pl.ds(j * size, size)] = low
-        return 0
-
-    lax.fori_loop(0, blocks, put_heavy, 0, unroll=True)
+    pair_copy.wait_recv()
+    ec[...] = em[pair] + ex[...]
+    cross_copy.start()
+    first = halo_copies(v_hbm, 0)
+    first[0].start()
+    first[1].start()
+    cross_copy.wait_send()
+    light_copies[1].start()
 
     base = r * group - REACH + total
 
@@ -270,45 +282,93 @@
         return big + small
 
     def heavy_products():
-        def one(i, _):
+        def one(i):
             cols = []
-            for j in range(heavy_slots):
-                own_col, peer_col = scalar(i, LIGHT + j)
+            for j in range(LIGHT, cap):
+                own_col, peer_col = cols_ref[i, j], colsp[i, j]
                 cols.append(peer_col + own_is_heavy * (own_col - peer_col))
             p_ref[i] = product(ea_ref[i], cols)
-            return 0
-
-        lax.fori_loop(0, blocks, one, 0, unroll=True)
-
-    def rows(half, source, older, target):
+
+        loop(blocks, one)
+
+    def place(half, i):
+        return pl.ds(pl.multiple_of((half * blocks + i) * size, size), size)
+
+    def rows(half, source, older, target, first_row=0, count=blocks, heavy=True):
         mine = y * half + (1 - y) * (1 - half)
         share = mine.astype(jnp.float32)
         flag = own_heavy * share + peer_heavy * (1.0 - share)
 
-        def one(i, _):
+        def one(i):
+            i = first_row + i
             cols = []
             for j in range(LIGHT):
-                own_col, peer_col = scalar(i, j)
+                own_col, peer_col = cols_ref[i, j], colsp[i, j]
                 cols.append(peer_col + mine * (own_col - peer_col))
-            image = product(a_ref[half * blocks + i], cols) + p_ref[i] * flag
-            at = pl.ds(pl.multiple_of((half * blocks + i) * size, size), size)
+            image = product(a_ref[half * blocks + i], cols)
+            if heavy:
+                image = image + p_ref[i] * flag
+            at = place(half, i)
             value = (image - CENTRE * source[at, :]) * (1.0 / HALF_WIDTH)
             if older is not None:
                 value = 2.0 * value - older[at, :]
             target[at, :] = value
-            return 0
-
-        lax.fori_loop(0, blocks, one, 0, unroll=True)
+
+        loop(count, one)
+
+    first[0].wait_recv()
+    first[1].wait_recv()
+    put_halo(0)
+    heavy_products()
+    rows(y, v_ref, None, y1)
+    second = halo_copies(y1, 1)
+
+    @pl.when(y == 1)
+    def _():
+        second[0].start()
+
+    @pl.when(y == 0)
+    def _():
+        second[1].start()
+
+    cross_copy.wait_recv()
+    pair_share.start()
+    chip_share.start()
+    light_copies[0].wait_recv()
+    put_light(hr, countsp, 1 - y, 0, half_rows)
+    rows(1 - y, v_ref, None, y1, 0, half_rows, False)
+    pair_share.wait_recv()
+    chip_share_2.start()
+    light_copies[1].wait_recv()
+    put_light(hr, countsp, 1 - y, half_rows, blocks - half_rows)
+    rows(1 - y, v_ref, None, y1, half_rows, blocks - half_rows, False)
+    chip_share.wait_recv()
+    chip_share_2.wait_recv()
+    put_heavy(True)
+    heavy_products()
+
+    def add_heavy(i):
+        at = place(1 - y, i)
+        y1[at, :] = y1[at, :] + p_ref[i] * (peer_heavy * (1.0 / HALF_WIDTH))
+
+    loop(blocks, add_heavy)
+
+    @pl.when(y == 0)
+    def _():
+        second[0].start()
+
+    @pl.when(y == 1)
+    def _():
+        second[1].start()
 
     chain = ((v_ref, None, y1), (y1, v_ref, y2), (y2, y1, out_ref))
-    started = [*first]
-    for step in range(ITERS):
+    started = [*first, *second]
+    for step in range(1, ITERS):
         source, older, target = chain[step]
-        if step:
-            put_window(source, 0, REACH, group)
-            started[2 * step].wait_recv()
-            started[2 * step + 1].wait_recv()
-            put_halo(step)
+        put_window(source, 0, REACH, group)
+        started[2 * step].wait_recv()
+        started[2 * step + 1].wait_recv()
+        put_halo(step)
         heavy_products()
         if step < ITERS - 1:
             following = halo_copies(target, step + 1)
@@ -342,7 +402,10 @@
     check_copy.wait_recv()
     chk_ref[...] = own_part + cs_r[...]
 
-    for copy in (cols_copy, counts_copy, light_copy, merge_copy, cross_copy, share_copy, check_copy, *started):
+    for copy in (
+        cols_copy, counts_copy, *light_copies, chip_copy, pair_copy, pair_share, chip_share,
+        chip_share_2, check_copy, *started,
+    ):
         copy.wait_send()
 
 
@@ -373,6 +436,9 @@
             pltpu.VMEM((blocks, LIGHT, size, size), f32),
             pltpu.VMEM((blocks // 2, heavy, size, size), f32),
             pltpu.VMEM((blocks // 2, heavy, size, size), f32),
+            pltpu.VMEM((blocks // 2, heavy, size, size), f32),
+            pltpu.VMEM((heavy, size, size), f32),
+            pltpu.VMEM((heavy, size, size), f32),
             pltpu.VMEM((blocks, heavy, size, size), f32),
             pltpu.SMEM((blocks, cap), jnp.int32),
             pltpu.SMEM((1, blocks), jnp.int32),
@@ -385,8 +451,8 @@
             pltpu.VMEM((ITERS, (REACH + RIGHT_REACH) * size, width), f32),
             pltpu.VMEM((1, blocks * size), f32),
             pltpu.VMEM((1, blocks * size), f32),
-            pltpu.SemaphoreType.DMA((7 + 2 * ITERS,)),
-            pltpu.SemaphoreType.DMA((7 + 2 * ITERS,)),
+            pltpu.SemaphoreType.DMA((11 + 2 * ITERS,)),
+            pltpu.SemaphoreType.DMA((11 + 2 * ITERS,)),
             pltpu.SemaphoreType.DMA((3,)),
         ],
         compiler_params=pltpu.CompilerParams(
@@ -405,7 +471,7 @@
         P(),
     )
     devices = mesh.shape["row"] * mesh.shape["col"]
-    one_heavy = devices < 64 and mesh.shape["col"] == 2 and mesh.shape["row"] >= 4 and mesh.shape["row"] % 2 == 0
+    one_heavy = devices < 64 and mesh.shape["col"] == 2 and mesh.shape["row"] >= 8 and mesh.shape["row"] % 4 == 0
     return jax.shard_map(
         columns_split if one_heavy else rows_split,
         mesh=mesh,

time: 61.7 us -> 59.6 us (0.966)
  the two profiles are of different devices: /device:TPU:10 before, /device:TPU:0 now
where the time goes in v3:
time: 59.6 us; the launch traced here: 59.4 us
  Pallas kernels  55.7 us (93%)
  local copies, waits for them, and re-layouts  3.12 us (5%)
  between operations  0.64 us (1%)
    pallas_call x1, Pallas kernels, columns_split(): pl.pallas_call(functools.partial(filter_kernel, rows_n), out_shape=(jax.S...  55.7 us
    unnamed x2, local copies, waits for them, and re-layouts  3.12 us

profile of v3, /device:TPU:0, one launch (start us, length us, event | category | flops | bytes accessed | tf_op | source)
XLA Modules:
  0.0 59.4 jit_solution(10767388390360361663)
XLA Ops:
  0.6 55.7 %shard_map.68 = (f32[1024,128]{1,0:T(8,128)}, f32[1,512]{1,0:T(1,128)}) custom-call(f32[1024,128]{1,0:T(8,128)} %v_hbm.1, f32[4,8,128,128]{3,2,1,0:T(8,128)} %h_ref.1, s32[4,8]{1,0:T(4,128)} %colsh_ref.1, s32[1,4]{1,0:T(1,128)} %bitcast.3, s32[4,8]{1,0:T(4,128)} %colsh_ref.1, s32[1,4]{1,0:T(1,128)} %bitcast.4, f32[1,256]{1,0:T(1,128)} %bitcast.6), custom_call_target="tpu_custom_call" | custom-call | tf_op jit(solution)/shard_map/pallas_call | solution.py:424
  56.3 1.9 %copy.9 = f32[1024,128]{1,0:T(8,128)} copy(f32[1024,128]{1,0:T(8,128)} %get-tuple-element.8) | data formatting | bytes 1048576
  58.2 1.3 %copy.10 = f32[512]{0:T(512)} copy(f32[512]{0:T(512)} %bitcast.5) | data formatting | bytes 4096

commit v4 on v3

--- a/solution.py
+++ b/solution.py
@@ -361,25 +361,42 @@
     def _():
         second[1].start()
 
+    def take_halo(half, copies, step):
+        @pl.when(half == 0)
+        def _():
+            copies[0].wait_recv()
+            put_window(halo.at[step], 0, 0, REACH)
+
+        @pl.when(half == 1)
+        def _():
+            copies[1].wait_recv()
+            put_window(halo.at[step], REACH * size, REACH + group, RIGHT_REACH)
+
+    def send_halo(half, copies):
+        @pl.when(half == 1)
+        def _():
+            copies[0].start()
+
+        @pl.when(half == 0)
+        def _():
+            copies[1].start()
+
     chain = ((v_ref, None, y1), (y1, v_ref, y2), (y2, y1, out_ref))
     started = [*first, *second]
+    early, late = 1 - y, y
     for step in range(1, ITERS):
         source, older, target = chain[step]
+        copies = started[2 * step:]
+        following = halo_copies(target, step + 1) if step < ITERS - 1 else ()
+        started += following
         put_window(source, 0, REACH, group)
-        started[2 * step].wait_recv()
-        started[2 * step + 1].wait_recv()
-        put_halo(step)
-        heavy_products()
-        if step < ITERS - 1:
-            following = halo_copies(target, step + 1)
-            started += following
-            rows(1, source, older, target)
-            following[0].start()
-            rows(0, source, older, target)
-            following[1].start()
-        else:
-            rows(1, source, older, target)
-            rows(0, source, older, target)
+        for half in (early, late):
+            take_halo(half, copies, step)
+            heavy_products()
+            rows(half, source, older, target)
+            if following:
+                send_halo(half, following)
+        early, late = late, early
 
     weight_copy.wait()
     weights = jnp.where(y == 0, w_ref[:, :size], w_ref[:, size:])

time: 59.6 us -> 59.3 us (level)
  no operation moved by 1% of the time
where the time goes in v4:
time: 59.3 us; the launch traced here: 59.1 us
  Pallas kernels  55.3 us (93%)
  local copies, waits for them, and re-layouts  3.12 us (5%)
  between operations  0.64 us (1%)
    pallas_call x1, Pallas kernels, columns_split(): pl.pallas_call(functools.partial(filter_kernel, rows_n), out_shape=(jax.S...  55.3 us
    unnamed x2, local copies, waits for them, and re-layouts  3.12 us

profile of v4, /device:TPU:0, one launch (start us, length us, event | category | flops | bytes accessed | tf_op | source)
XLA Modules:
  0.0 59.1 jit_solution(3539662292748350072)
XLA Ops:
  0.6 55.3 %shard_map.68 = (f32[1024,128]{1,0:T(8,128)}, f32[1,512]{1,0:T(1,128)}) custom-call(f32[1024,128]{1,0:T(8,128)} %v_hbm.1, f32[4,8,128,128]{3,2,1,0:T(8,128)} %h_ref.1, s32[4,8]{1,0:T(4,128)} %colsh_ref.1, s32[1,4]{1,0:T(1,128)} %bitcast.3, s32[4,8]{1,0:T(4,128)} %colsh_ref.1, s32[1,4]{1,0:T(1,128)} %bitcast.4, f32[1,256]{1,0:T(1,128)} %bitcast.6), custom_call_target="tpu_custom_call" | custom-call | tf_op jit(solution)/shard_map/pallas_call | solution.py:441
  56.0 1.9 %copy.9 = f32[1024,128]{1,0:T(8,128)} copy(f32[1024,128]{1,0:T(8,128)} %get-tuple-element.8) | data formatting | bytes 1048576
  57.8 1.3 %copy.10 = f32[512]{0:T(512)} copy(f32[512]{0:T(512)} %bitcast.5) | data formatting | bytes 4096

commit v5 on v4

--- a/solution.py
+++ b/solution.py
@@ -158,28 +158,39 @@
     cols_copy = remote(colsh_ref, colsp, 0, peer)
     counts_copy = remote(countsh_ref, countsp, 1, peer)
 
-    def light_part(part):
-        at = pl.ds(half_rows * part, half_rows)
+    def light_part(part, first_row, count):
+        at = pl.ds(first_row, count)
         return remote(h_ref.at[at, pl.ds(0, LIGHT)], hr.at[at], 2 + part, peer)
 
-    light_copies = (light_part(0), light_part(1))
+    lead = blocks - 1
+    light_copies = (light_part(0, 0, lead), light_part(1, lead, 1))
     chip_copy = remote(st, es, 4, sibling)
-    pair_copy = remote(em.at[1 - pair], ex, 5, across)
-    cross_copy = remote(ec, er.at[mine_row], 6, peer)
-    pair_share = remote(er.at[mine_row], er.at[mine_row], 7, across)
-    chip_share = remote(er.at[mine_row], er.at[mine_row], 8, sibling)
-    chip_share_2 = remote(er.at[other_row], er.at[other_row], 9, sibling)
-    check_copy = remote(cs_s, cs_r, 10, peer)
+    pieces = 2
+    piece = size // pieces
+
+    def pieced(src, dst, index, target):
+        copies = []
+        for k in range(pieces):
+            at = pl.ds(k * piece, piece)
+            copies.append(remote(src.at[:, at], dst.at[:, at], index + k, target))
+        return copies
+
+    pair_copies = pieced(em.at[1 - pair], ex, 5, across)
+    cross_copies = pieced(ec, er.at[mine_row], 7, peer)
+    pair_shares = pieced(er.at[mine_row], er.at[mine_row], 9, across)
+    chip_shares = pieced(er.at[mine_row], er.at[mine_row], 11, sibling)
+    chip_shares_2 = pieced(er.at[other_row], er.at[other_row], 13, sibling)
+    check_copy = remote(cs_s, cs_r, 15, peer)
 
     def halo_copies(source, step):
         own_rows = group * size
         to_right = remote(
             source.at[pl.ds(own_rows - REACH * size, REACH * size)],
-            halo.at[step, pl.ds(0, REACH * size)], 11 + 2 * step, {"row": right},
+            halo.at[step, pl.ds(0, REACH * size)], 16 + 2 * step, {"row": right},
         )
         to_left = remote(
             source.at[pl.ds(0, RIGHT_REACH * size)],
-            halo.at[step, pl.ds(REACH * size, RIGHT_REACH * size)], 12 + 2 * step, {"row": left},
+            halo.at[step, pl.ds(REACH * size, RIGHT_REACH * size)], 17 + 2 * step, {"row": left},
         )
         return to_right, to_left
 
@@ -251,7 +262,8 @@
         em[i] = hv[half_rows * core + i, pl.ds(LIGHT, heavy_slots)] * own_heavy + es[i]
 
     loop(half_rows, merge)
-    pair_copy.start()
+    for copy in pair_copies:
+        copy.start()
 
     put_heavy(False)
     vector_copy.wait()
@@ -260,14 +272,14 @@
     counts_copy.wait_recv()
     peer_heavy = beyond(countsp[0, 0], LIGHT).astype(jnp.float32)
 
-    pair_copy.wait_recv()
-    ec[...] = em[pair] + ex[...]
-    cross_copy.start()
+    for k in range(pieces):
+        pair_copies[k].wait_recv()
+        at = pl.ds(k * piece, piece)
+        ec[:, at, :] = em[pair, :, at, :] + ex[:, at, :]
+        cross_copies[k].start()
     first = halo_copies(v_hbm, 0)
     first[0].start()
     first[1].start()
-    cross_copy.wait_send()
-    light_copies[1].start()
 
     base = r * group - REACH + total
 
@@ -316,34 +328,41 @@
 
         loop(count, one)
 
+    def share(k):
+        cross_copies[k].wait_recv()
+        pair_shares[k].start()
+        chip_shares[k].start()
+
+    share(0)
     first[0].wait_recv()
     first[1].wait_recv()
     put_halo(0)
     heavy_products()
     rows(y, v_ref, None, y1)
+    share(1)
+    for copy in cross_copies:
+        copy.wait_send()
+    light_copies[1].start()
     second = halo_copies(y1, 1)
 
-    @pl.when(y == 1)
-    def _():
-        second[0].start()
-
-    @pl.when(y == 0)
-    def _():
-        second[1].start()
-
-    cross_copy.wait_recv()
-    pair_share.start()
-    chip_share.start()
+    def send_halo(half, copies):
+        @pl.when(half == 1)
+        def _():
+            copies[0].start()
+
+        @pl.when(half == 0)
+        def _():
+            copies[1].start()
+
+    send_halo(y, second)
     light_copies[0].wait_recv()
-    put_light(hr, countsp, 1 - y, 0, half_rows)
-    rows(1 - y, v_ref, None, y1, 0, half_rows, False)
-    pair_share.wait_recv()
-    chip_share_2.start()
-    light_copies[1].wait_recv()
-    put_light(hr, countsp, 1 - y, half_rows, blocks - half_rows)
-    rows(1 - y, v_ref, None, y1, half_rows, blocks - half_rows, False)
-    chip_share.wait_recv()
-    chip_share_2.wait_recv()
+    put_light(hr, countsp, 1 - y, 0, lead)
+    rows(1 - y, v_ref, None, y1, 0, lead, False)
+    for k in range(pieces):
+        pair_shares[k].wait_recv()
+        chip_shares_2[k].start()
+    for copy in (*chip_shares, *chip_shares_2):
+        copy.wait_recv()
     put_heavy(True)
     heavy_products()
 
@@ -351,15 +370,11 @@
         at = place(1 - y, i)
         y1[at, :] = y1[at, :] + p_ref[i] * (peer_heavy * (1.0 / HALF_WIDTH))
 
-    loop(blocks, add_heavy)
-
-    @pl.when(y == 0)
-    def _():
-        second[0].start()
-
-    @pl.when(y == 1)
-    def _():
-        second[1].start()
+    loop(lead, add_heavy)
+    light_copies[1].wait_recv()
+    put_light(hr, countsp, 1 - y, lead, 1)
+    rows(1 - y, v_ref, None, y1, lead, 1)
+    send_halo(1 - y, second)
 
     def take_halo(half, copies, step):
         @pl.when(half == 0)
@@ -371,15 +386,6 @@
         def _():
             copies[1].wait_recv()
             put_window(halo.at[step], REACH * size, REACH + group, RIGHT_REACH)
-
-    def send_halo(half, copies):
-        @pl.when(half == 1)
-        def _():
-            copies[0].start()
-
-        @pl.when(half == 0)
-        def _():
-            copies[1].start()
 
     chain = ((v_ref, None, y1), (y1, v_ref, y2), (y2, y1, out_ref))
     started = [*first, *second]
@@ -420,8 +426,8 @@
     chk_ref[...] = own_part + cs_r[...]
 
     for copy in (
-        cols_copy, counts_copy, *light_copies, chip_copy, pair_copy, pair_share, chip_share,
-        chip_share_2, check_copy, *started,
+        cols_copy, counts_copy, *light_copies, chip_copy, *pair_copies, *pair_shares, *chip_shares,
+        *chip_shares_2, check_copy, *started,
     ):
         copy.wait_send()
 
@@ -468,8 +474,8 @@
             pltpu.VMEM((ITERS, (REACH + RIGHT_REACH) * size, width), f32),
             pltpu.VMEM((1, blocks * size), f32),
             pltpu.VMEM((1, blocks * size), f32),
-            pltpu.SemaphoreType.DMA((11 + 2 * ITERS,)),
-            pltpu.SemaphoreType.DMA((11 + 2 * ITERS,)),
+            pltpu.SemaphoreType.DMA((16 + 2 * ITERS,)),
+            pltpu.SemaphoreType.DMA((16 + 2 * ITERS,)),
             pltpu.SemaphoreType.DMA((3,)),
         ],
         compiler_params=pltpu.CompilerParams(

time: 59.3 us -> 56.5 us (0.953)
  Pallas kernels: 55.3 us -> 52.5 us
    pallas_call x1, Pallas kernels: 55.3 us -> 52.5 us  [columns_split(): pl.pallas_call(functools.partial(filter_kernel, rows_n), out_shape=(jax.S...]
where the time goes in v5:
time: 56.5 us; the launch traced here: 56.3 us
  Pallas kernels  52.5 us (93%)
  local copies, waits for them, and re-layouts  3.12 us (6%)
  between operations  0.64 us (1%)
    pallas_call x1, Pallas kernels, columns_split(): pl.pallas_call(functools.partial(filter_kernel, rows_n), out_shape=(jax.S...  52.5 us
    unnamed x2, local copies, waits for them, and re-layouts  3.12 us

profile of v5, /device:TPU:0, one launch (start us, length us, event | category | flops | bytes accessed | tf_op | source)
XLA Modules:
  0.0 56.3 jit_solution(10183419640719870699)
XLA Ops:
  0.6 52.5 %shard_map.68 = (f32[1024,128]{1,0:T(8,128)}, f32[1,512]{1,0:T(1,128)}) custom-call(f32[1024,128]{1,0:T(8,128)} %v_hbm.1, f32[4,8,128,128]{3,2,1,0:T(8,128)} %h_ref.1, s32[4,8]{1,0:T(4,128)} %colsh_ref.1, s32[1,4]{1,0:T(1,128)} %bitcast.3, s32[4,8]{1,0:T(4,128)} %colsh_ref.1, s32[1,4]{1,0:T(1,128)} %bitcast.4, f32[1,256]{1,0:T(1,128)} %bitcast.6), custom_call_target="tpu_custom_call" | custom-call | tf_op jit(solution)/shard_map/pallas_call | solution.py:447
  53.2 1.9 %copy.9 = f32[1024,128]{1,0:T(8,128)} copy(f32[1024,128]{1,0:T(8,128)} %get-tuple-element.8) | data formatting | bytes 1048576
  55.0 1.3 %copy.10 = f32[512]{0:T(512)} copy(f32[512]{0:T(512)} %bitcast.5) | data formatting | bytes 4096

commit v6 on v5

--- a/solution.py
+++ b/solution.py
@@ -118,14 +118,14 @@
 
 def filter_kernel(
     rows_n, v_hbm, h_ref, cols_ref, counts_ref, colsh_ref, countsh_ref, w_hbm, out_ref, chk_ref,
-    v_ref, w_ref, hv, hr, st, es, em, ex, ec, er, colsp, countsp, a_ref, ea_ref, win, p_ref, y1, y2,
+    v_ref, w_ref, hv, hr, st, es, em, ex, ec, er, colsp, countsp, a_ref, win, y1, y2,
     halo, cs_s, cs_r, send, recv, loc,
 ):
     r = lax.axis_index("row")
     y = lax.axis_index("col")
     right, left = lax.rem(r + 1, rows_n), lax.rem(r + rows_n - 1, rows_n)
     core = lax.rem(r, 2)
-    pair = lax.rem(r // 2, 2)
+    sides = (lax.rem(r // 2, 2), lax.rem(r // 4, 2))
     blocks, cap, size, _ = hv.shape
     group = 2 * blocks
     total = rows_n * group
@@ -133,10 +133,10 @@
     half_rows = blocks // 2
     peer = {"col": 1 - y}
     sibling = {"row": r + 1 - 2 * core}
-    across = {"row": r + 2 - 4 * pair}
+    across = ({"row": r + 2 - 4 * sides[0]}, {"row": r + 4 - 8 * sides[1]})
 
     barrier = pltpu.get_barrier_semaphore()
-    for target in ({"row": left}, {"row": right}, across, peer):
+    for target in ({"row": left}, {"row": right}, *across, peer):
         pl.semaphore_signal(barrier, inc=1, device_id=target, device_id_type=MESH)
 
     own_copy = pltpu.make_async_copy(h_ref, hv, loc.at[0])
@@ -145,7 +145,7 @@
     own_copy.start()
     vector_copy.start()
     weight_copy.start()
-    pl.semaphore_wait(barrier, 4)
+    pl.semaphore_wait(barrier, 5)
 
     def remote(src, dst, index, target):
         return pltpu.make_async_remote_copy(
@@ -153,8 +153,8 @@
             device_id=target, device_id_type=MESH,
         )
 
-    mine_row = half_rows * core + pair
-    other_row = half_rows * core + 1 - pair
+    mine_rows = [half_rows * core + side for side in sides]
+    other_rows = [half_rows * core + 1 - side for side in sides]
     cols_copy = remote(colsh_ref, colsp, 0, peer)
     counts_copy = remote(countsh_ref, countsp, 1, peer)
 
@@ -165,21 +165,26 @@
     lead = blocks - 1
     light_copies = (light_part(0, 0, lead), light_part(1, lead, 1))
     chip_copy = remote(st, es, 4, sibling)
-    pieces = 2
+    pieces = len(sides)
     piece = size // pieces
-
-    def pieced(src, dst, index, target):
+    spans = [pl.ds(k * piece, piece) for k in range(pieces)]
+
+    def shares(rows_of, index, targets):
         copies = []
         for k in range(pieces):
-            at = pl.ds(k * piece, piece)
-            copies.append(remote(src.at[:, at], dst.at[:, at], index + k, target))
+            part = er.at[rows_of[k], :, spans[k]]
+            copies.append(remote(part, part, index + k, targets[k]))
         return copies
 
-    pair_copies = pieced(em.at[1 - pair], ex, 5, across)
-    cross_copies = pieced(ec, er.at[mine_row], 7, peer)
-    pair_shares = pieced(er.at[mine_row], er.at[mine_row], 9, across)
-    chip_shares = pieced(er.at[mine_row], er.at[mine_row], 11, sibling)
-    chip_shares_2 = pieced(er.at[other_row], er.at[other_row], 13, sibling)
+    pair_copies = [
+        remote(em.at[1 - sides[k], :, spans[k]], ex.at[:, spans[k]], 5 + k, across[k]) for k in range(pieces)
+    ]
+    cross_copies = [
+        remote(ec.at[:, spans[k]], er.at[mine_rows[k], :, spans[k]], 7 + k, peer) for k in range(pieces)
+    ]
+    pair_shares = shares(mine_rows, 9, across)
+    chip_shares = shares(mine_rows, 11, [sibling] * pieces)
+    chip_shares_2 = shares(other_rows, 13, [sibling] * pieces)
     check_copy = remote(cs_s, cs_r, 15, peer)
 
     def halo_copies(source, step):
@@ -218,8 +223,7 @@
         put_window(halo.at[step], 0, 0, REACH)
         put_window(halo.at[step], REACH * size, REACH + group, RIGHT_REACH)
 
-    own_is_heavy = beyond(counts_ref[0, 0], LIGHT)
-    own_heavy = own_is_heavy.astype(jnp.float32)
+    own_heavy = beyond(counts_ref[0, 0], LIGHT).astype(jnp.float32)
 
     own_copy.wait()
 
@@ -229,33 +233,20 @@
     loop(half_rows, stage)
     chip_copy.start()
 
-    def put_light(source, table, half, first_row, count):
+    def put_slots(source, source_slot, table, half, first_row, count, slots):
         def one(i):
             i = first_row + i
             live_count = table[0, i]
-            for j in range(LIGHT):
+            for j in slots:
                 live = beyond(live_count, j).astype(jnp.float32)
-                high, low = split2(source[i, j] * live)
+                high, low = split2(source[i, j - source_slot] * live)
                 a_ref[half * blocks + i, pl.ds(0, size), pl.ds(j * size, size)] = high
                 a_ref[half * blocks + i, pl.ds(size, size), pl.ds(j * size, size)] = low
 
         loop(count, one)
 
-    def put_heavy(with_peer):
-        def one(i):
-            for j in range(heavy_slots):
-                live = beyond(counts_ref[0, i], LIGHT + j).astype(jnp.float32)
-                value = hv[i, LIGHT + j] * live
-                if with_peer:
-                    live = beyond(countsp[0, i], LIGHT + j).astype(jnp.float32) * (1.0 - own_heavy)
-                    value = value + er[i, j] * live
-                high, low = split2(value)
-                ea_ref[i, pl.ds(0, size), pl.ds(j * size, size)] = high
-                ea_ref[i, pl.ds(size, size), pl.ds(j * size, size)] = low
-
-        loop(blocks, one)
-
-    put_light(hv, counts_ref, y, 0, blocks)
+    light_slots, more_slots, all_slots = range(LIGHT), range(LIGHT, cap), range(cap)
+    put_slots(hv, 0, counts_ref, y, 0, blocks, light_slots)
     chip_copy.wait_recv()
 
     def merge(i):
@@ -265,17 +256,16 @@
     for copy in pair_copies:
         copy.start()
 
-    put_heavy(False)
+    put_slots(hv, 0, counts_ref, y, 0, blocks, more_slots)
     vector_copy.wait()
     put_window(v_ref, 0, REACH, group)
     cols_copy.wait_recv()
     counts_copy.wait_recv()
-    peer_heavy = beyond(countsp[0, 0], LIGHT).astype(jnp.float32)
 
     for k in range(pieces):
         pair_copies[k].wait_recv()
-        at = pl.ds(k * piece, piece)
-        ec[:, at, :] = em[pair, :, at, :] + ex[:, at, :]
+        at = spans[k]
+        ec[:, at, :] = em[sides[k], :, at, :] + ex[:, at, :]
         cross_copies[k].start()
     first = halo_copies(v_hbm, 0)
     first[0].start()
@@ -293,33 +283,22 @@
         small = full[:size, size:] + full[size:, :size] + full[size:, size:]
         return big + small
 
-    def heavy_products():
-        def one(i):
-            cols = []
-            for j in range(LIGHT, cap):
-                own_col, peer_col = cols_ref[i, j], colsp[i, j]
-                cols.append(peer_col + own_is_heavy * (own_col - peer_col))
-            p_ref[i] = product(ea_ref[i], cols)
-
-        loop(blocks, one)
-
     def place(half, i):
         return pl.ds(pl.multiple_of((half * blocks + i) * size, size), size)
 
-    def rows(half, source, older, target, first_row=0, count=blocks, heavy=True):
+    def image_of(half, i, slots):
         mine = y * half + (1 - y) * (1 - half)
-        share = mine.astype(jnp.float32)
-        flag = own_heavy * share + peer_heavy * (1.0 - share)
-
+        cols = []
+        for j in slots:
+            own_col, peer_col = cols_ref[i, j], colsp[i, j]
+            cols.append(peer_col + mine * (own_col - peer_col))
+        lanes = pl.ds(slots[0] * size, len(slots) * size)
+        return product(a_ref[half * blocks + i, :, lanes], cols)
+
+    def rows(half, source, older, target, first_row=0, count=blocks, slots=all_slots):
         def one(i):
             i = first_row + i
-            cols = []
-            for j in range(LIGHT):
-                own_col, peer_col = cols_ref[i, j], colsp[i, j]
-                cols.append(peer_col + mine * (own_col - peer_col))
-            image = product(a_ref[half * blocks + i], cols)
-            if heavy:
-                image = image + p_ref[i] * flag
+            image = image_of(half, i, slots)
             at = place(half, i)
             value = (image - CENTRE * source[at, :]) * (1.0 / HALF_WIDTH)
             if older is not None:
@@ -337,7 +316,6 @@
     first[0].wait_recv()
     first[1].wait_recv()
     put_halo(0)
-    heavy_products()
     rows(y, v_ref, None, y1)
     share(1)
     for copy in cross_copies:
@@ -356,23 +334,22 @@
 
     send_halo(y, second)
     light_copies[0].wait_recv()
-    put_light(hr, countsp, 1 - y, 0, lead)
-    rows(1 - y, v_ref, None, y1, 0, lead, False)
+    put_slots(hr, 0, countsp, 1 - y, 0, lead, light_slots)
+    rows(1 - y, v_ref, None, y1, 0, lead, light_slots)
     for k in range(pieces):
         pair_shares[k].wait_recv()
         chip_shares_2[k].start()
     for copy in (*chip_shares, *chip_shares_2):
         copy.wait_recv()
-    put_heavy(True)
-    heavy_products()
+    put_slots(er, LIGHT, countsp, 1 - y, 0, blocks, more_slots)
 
     def add_heavy(i):
         at = place(1 - y, i)
-        y1[at, :] = y1[at, :] + p_ref[i] * (peer_heavy * (1.0 / HALF_WIDTH))
+        y1[at, :] = y1[at, :] + image_of(1 - y, i, more_slots) * (1.0 / HALF_WIDTH)
 
     loop(lead, add_heavy)
     light_copies[1].wait_recv()
-    put_light(hr, countsp, 1 - y, lead, 1)
+    put_slots(hr, 0, countsp, 1 - y, lead, 1, light_slots)
     rows(1 - y, v_ref, None, y1, lead, 1)
     send_halo(1 - y, second)
 
@@ -398,7 +375,6 @@
         put_window(source, 0, REACH, group)
         for half in (early, late):
             take_halo(half, copies, step)
-            heavy_products()
             rows(half, source, older, target)
             if following:
                 send_halo(half, following)
@@ -465,10 +441,8 @@
             pltpu.VMEM((blocks, heavy, size, size), f32),
             pltpu.SMEM((blocks, cap), jnp.int32),
             pltpu.SMEM((1, blocks), jnp.int32),
-            pltpu.VMEM((group, 2 * size, LIGHT * size), bf16),
-            pltpu.VMEM((blocks, 2 * size, heavy * size), bf16),
+            pltpu.VMEM((group, 2 * size, cap * size), bf16),
             pltpu.VMEM((window, size, 2 * width), bf16),
-            pltpu.VMEM((blocks, size, width), f32),
             pltpu.VMEM((height, width), f32),
             pltpu.VMEM((height, width), f32),
             pltpu.VMEM((ITERS, (REACH + RIGHT_REACH) * size, width), f32),
@@ -494,7 +468,7 @@
         P(),
     )
     devices = mesh.shape["row"] * mesh.shape["col"]
-    one_heavy = devices < 64 and mesh.shape["col"] == 2 and mesh.shape["row"] >= 8 and mesh.shape["row"] % 4 == 0
+    one_heavy = devices < 64 and mesh.shape["col"] == 2 and mesh.shape["row"] >= 16 and mesh.shape["row"] % 8 == 0
     return jax.shard_map(
         columns_split if one_heavy else rows_split,
         mesh=mesh,

time: 56.5 us -> 54.2 us (0.959)
  Pallas kernels: 52.5 us -> 50.2 us
    pallas_call x1, Pallas kernels: 52.5 us -> 50.2 us  [columns_split(): pl.pallas_call(functools.partial(filter_kernel, rows_n), out_shape=(jax.S...]
where the time goes in v6:
time: 54.2 us; the launch traced here: 54 us
  Pallas kernels  50.2 us (93%)
  local copies, waits for them, and re-layouts  3.12 us (6%)
  between operations  0.64 us (1%)
    pallas_call x1, Pallas kernels, columns_split(): pl.pallas_call(functools.partial(filter_kernel, rows_n), out_shape=(jax.S...  50.2 us
    unnamed x2, local copies, waits for them, and re-layouts  3.12 us

profile of v6, /device:TPU:0, one launch (start us, length us, event | category | flops | bytes accessed | tf_op | source)
XLA Modules:
  0.0 54.0 jit_solution(10888637230580918485)
XLA Ops:
  0.6 50.2 %shard_map.68 = (f32[1024,128]{1,0:T(8,128)}, f32[1,512]{1,0:T(1,128)}) custom-call(f32[1024,128]{1,0:T(8,128)} %v_hbm.1, f32[4,8,128,128]{3,2,1,0:T(8,128)} %h_ref.1, s32[4,8]{1,0:T(4,128)} %colsh_ref.1, s32[1,4]{1,0:T(1,128)} %bitcast.3, s32[4,8]{1,0:T(4,128)} %colsh_ref.1, s32[1,4]{1,0:T(1,128)} %bitcast.4, f32[1,256]{1,0:T(1,128)} %bitcast.6), custom_call_target="tpu_custom_call" | custom-call | tf_op jit(solution)/shard_map/pallas_call | solution.py:423
  50.9 1.9 %copy.9 = f32[1024,128]{1,0:T(8,128)} copy(f32[1024,128]{1,0:T(8,128)} %get-tuple-element.8) | data formatting | bytes 1048576
  52.7 1.3 %copy.10 = f32[512]{0:T(512)} copy(f32[512]{0:T(512)} %bitcast.5) | data formatting | bytes 4096

commit v7 on v6

--- a/solution.py
+++ b/solution.py
@@ -117,8 +117,8 @@
 
 
 def filter_kernel(
-    rows_n, v_hbm, h_ref, cols_ref, counts_ref, colsh_ref, countsh_ref, w_hbm, out_ref, chk_ref,
-    v_ref, w_ref, hv, hr, st, es, em, ex, ec, er, colsp, countsp, a_ref, win, y1, y2,
+    rows_n, v_hbm, h_ref, cols_ref, counts_ref, colsh_ref, countsh_ref, w_hbm, out_hbm, chk_ref,
+    v_ref, w_ref, out_ref, hv, hr, st, es, em, ex, ec, er, colsp, countsp, a_ref, win, y1, y2,
     halo, cs_s, cs_r, send, recv, loc,
 ):
     r = lax.axis_index("row")
@@ -255,6 +255,9 @@
     loop(half_rows, merge)
     for copy in pair_copies:
         copy.start()
+    first = halo_copies(v_hbm, 0)
+    first[0].start()
+    first[1].start()
 
     put_slots(hv, 0, counts_ref, y, 0, blocks, more_slots)
     vector_copy.wait()
@@ -267,9 +270,6 @@
         at = spans[k]
         ec[:, at, :] = em[sides[k], :, at, :] + ex[:, at, :]
         cross_copies[k].start()
-    first = halo_copies(v_hbm, 0)
-    first[0].start()
-    first[1].start()
 
     base = r * group - REACH + total
 
@@ -312,27 +312,27 @@
         pair_shares[k].start()
         chip_shares[k].start()
 
-    share(0)
     first[0].wait_recv()
     first[1].wait_recv()
     put_halo(0)
     rows(y, v_ref, None, y1)
+    second = halo_copies(y1, 1)
+
+    def send_halo(half, copies):
+        @pl.when(half == 1)
+        def _():
+            copies[0].start()
+
+        @pl.when(half == 0)
+        def _():
+            copies[1].start()
+
+    send_halo(y, second)
+    share(0)
     share(1)
     for copy in cross_copies:
         copy.wait_send()
     light_copies[1].start()
-    second = halo_copies(y1, 1)
-
-    def send_halo(half, copies):
-        @pl.when(half == 1)
-        def _():
-            copies[0].start()
-
-        @pl.when(half == 0)
-        def _():
-            copies[1].start()
-
-    send_halo(y, second)
     light_copies[0].wait_recv()
     put_slots(hr, 0, countsp, 1 - y, 0, lead, light_slots)
     rows(1 - y, v_ref, None, y1, 0, lead, light_slots)
@@ -367,6 +367,7 @@
     chain = ((v_ref, None, y1), (y1, v_ref, y2), (y2, y1, out_ref))
     started = [*first, *second]
     early, late = 1 - y, y
+    out_copies = []
     for step in range(1, ITERS):
         source, older, target = chain[step]
         copies = started[2 * step:]
@@ -378,6 +379,10 @@
             rows(half, source, older, target)
             if following:
                 send_halo(half, following)
+            else:
+                at = pl.ds(pl.multiple_of(half * blocks * size, size), blocks * size)
+                out_copies.append(pltpu.make_async_copy(out_ref.at[at], out_hbm.at[at], loc.at[3 + len(out_copies)]))
+                out_copies[-1].start()
         early, late = late, early
 
     weight_copy.wait()
@@ -406,6 +411,8 @@
         *chip_shares_2, check_copy, *started,
     ):
         copy.wait_send()
+    for copy in out_copies:
+        copy.wait()
 
 
 def columns_split(start_vectors, ham_blocks, block_cols, block_counts, check_weights):
@@ -427,10 +434,11 @@
             jax.ShapeDtypeStruct((1, blocks * size), f32),
         ),
         in_specs=[anywhere, anywhere, smem, smem, anywhere, anywhere, anywhere],
-        out_specs=(vmem, vmem),
+        out_specs=(anywhere, vmem),
         scratch_shapes=[
             pltpu.VMEM((height, width), f32),
             pltpu.VMEM((1, 2 * width), f32),
+            pltpu.VMEM((height, width), f32),
             pltpu.VMEM((blocks, cap, size, size), f32),
             pltpu.VMEM((blocks, LIGHT, size, size), f32),
             pltpu.VMEM((blocks // 2, heavy, size, size), f32),
@@ -450,7 +458,7 @@
             pltpu.VMEM((1, blocks * size), f32),
             pltpu.SemaphoreType.DMA((16 + 2 * ITERS,)),
             pltpu.SemaphoreType.DMA((16 + 2 * ITERS,)),
-            pltpu.SemaphoreType.DMA((3,)),
+            pltpu.SemaphoreType.DMA((5,)),
         ],
         compiler_params=pltpu.CompilerParams(
             collective_id=0, has_side_effects=True, vmem_limit_bytes=60 * 1024 * 1024

time: 54.2 us -> 54 us (level)
  no operation moved by 1% of the time
where the time goes in v7:
time: 54 us; the launch traced here: 53.8 us
  Pallas kernels  50.1 us (93%)
  local copies, waits for them, and re-layouts  3.12 us (6%)
  between operations  0.64 us (1%)
    pallas_call x1, Pallas kernels, columns_split(): pl.pallas_call(functools.partial(filter_kernel, rows_n), out_shape=(jax.S...  50.1 us
    unnamed x2, local copies, waits for them, and re-layouts  3.12 us

profile of v7, /device:TPU:0, one launch (start us, length us, event | category | flops | bytes accessed | tf_op | source)
XLA Modules:
  0.0 53.8 jit_solution(12432395974611497026)
XLA Ops:
  0.6 50.1 %shard_map.68 = (f32[1024,128]{1,0:T(8,128)}, f32[1,512]{1,0:T(1,128)}) custom-call(f32[1024,128]{1,0:T(8,128)} %v_hbm.1, f32[4,8,128,128]{3,2,1,0:T(8,128)} %h_ref.1, s32[4,8]{1,0:T(4,128)} %colsh_ref.1, s32[1,4]{1,0:T(1,128)} %bitcast.3, s32[4,8]{1,0:T(4,128)} %colsh_ref.1, s32[1,4]{1,0:T(1,128)} %bitcast.4, f32[1,256]{1,0:T(1,128)} %bitcast.6), custom_call_target="tpu_custom_call" | custom-call | tf_op jit(solution)/shard_map/pallas_call | solution.py:430
  50.7 1.9 %copy.9 = f32[1024,128]{1,0:T(8,128)} copy(f32[1024,128]{1,0:T(8,128)} %get-tuple-element.8) | data formatting | bytes 1048576
  52.6 1.3 %copy.10 = f32[512]{0:T(512)} copy(f32[512]{0:T(512)} %bitcast.5) | data formatting | bytes 4096

commit v8 on v7

--- a/solution.py
+++ b/solution.py
@@ -188,15 +188,20 @@
     check_copy = remote(cs_s, cs_r, 15, peer)
 
     def halo_copies(source, step):
-        own_rows = group * size
-        to_right = remote(
-            source.at[pl.ds(own_rows - REACH * size, REACH * size)],
-            halo.at[step, pl.ds(0, REACH * size)], 16 + 2 * step, {"row": right},
-        )
-        to_left = remote(
-            source.at[pl.ds(0, RIGHT_REACH * size)],
-            halo.at[step, pl.ds(REACH * size, RIGHT_REACH * size)], 17 + 2 * step, {"row": left},
-        )
+        own_rows = (group - REACH) * size
+        to_right, to_left = [], []
+        for part in range(2):
+            at = part * half_rows * size
+            count = half_rows * size
+            to_right.append(remote(
+                source.at[pl.ds(own_rows + at, count)], halo.at[step, pl.ds(at, count)],
+                16 + 4 * step + part, {"row": right},
+            ))
+            count = min(count, RIGHT_REACH * size - at)
+            to_left.append(remote(
+                source.at[pl.ds(at, count)], halo.at[step, pl.ds(REACH * size + at, count)],
+                18 + 4 * step + part, {"row": left},
+            ))
         return to_right, to_left
 
     cols_copy.start()
@@ -256,8 +261,8 @@
     for copy in pair_copies:
         copy.start()
     first = halo_copies(v_hbm, 0)
-    first[0].start()
-    first[1].start()
+    for copy in (*first[0], *first[1]):
+        copy.start()
 
     put_slots(hv, 0, counts_ref, y, 0, blocks, more_slots)
     vector_copy.wait()
@@ -312,22 +317,23 @@
         pair_shares[k].start()
         chip_shares[k].start()
 
-    first[0].wait_recv()
-    first[1].wait_recv()
+    for copy in (*first[0], *first[1]):
+        copy.wait_recv()
     put_halo(0)
     rows(y, v_ref, None, y1)
     second = halo_copies(y1, 1)
 
-    def send_halo(half, copies):
+    def send_halo(half, copies, part):
         @pl.when(half == 1)
         def _():
-            copies[0].start()
+            copies[0][part].start()
 
         @pl.when(half == 0)
         def _():
-            copies[1].start()
-
-    send_halo(y, second)
+            copies[1][part].start()
+
+    send_halo(y, second, 0)
+    send_halo(y, second, 1)
     share(0)
     share(1)
     for copy in cross_copies:
@@ -348,20 +354,23 @@
         y1[at, :] = y1[at, :] + image_of(1 - y, i, more_slots) * (1.0 / HALF_WIDTH)
 
     loop(lead, add_heavy)
+    send_halo(1 - y, second, 0)
     light_copies[1].wait_recv()
     put_slots(hr, 0, countsp, 1 - y, lead, 1, light_slots)
     rows(1 - y, v_ref, None, y1, lead, 1)
-    send_halo(1 - y, second)
+    send_halo(1 - y, second, 1)
 
     def take_halo(half, copies, step):
         @pl.when(half == 0)
         def _():
-            copies[0].wait_recv()
+            copies[0][0].wait_recv()
+            copies[0][1].wait_recv()
             put_window(halo.at[step], 0, 0, REACH)
 
         @pl.when(half == 1)
         def _():
-            copies[1].wait_recv()
+            copies[1][0].wait_recv()
+            copies[1][1].wait_recv()
             put_window(halo.at[step], REACH * size, REACH + group, RIGHT_REACH)
 
     chain = ((v_ref, None, y1), (y1, v_ref, y2), (y2, y1, out_ref))
@@ -376,10 +385,12 @@
         put_window(source, 0, REACH, group)
         for half in (early, late):
             take_halo(half, copies, step)
-            rows(half, source, older, target)
             if following:
-                send_halo(half, following)
+                for part in range(2):
+                    rows(half, source, older, target, part * half_rows, half_rows)
+                    send_halo(half, following, part)
             else:
+                rows(half, source, older, target)
                 at = pl.ds(pl.multiple_of(half * blocks * size, size), blocks * size)
                 out_copies.append(pltpu.make_async_copy(out_ref.at[at], out_hbm.at[at], loc.at[3 + len(out_copies)]))
                 out_copies[-1].start()
@@ -408,7 +419,7 @@
 
     for copy in (
         cols_copy, counts_copy, *light_copies, chip_copy, *pair_copies, *pair_shares, *chip_shares,
-        *chip_shares_2, check_copy, *started,
+        *chip_shares_2, check_copy, *(copy for side in started for copy in side),
     ):
         copy.wait_send()
     for copy in out_copies:
@@ -456,8 +467,8 @@
             pltpu.VMEM((ITERS, (REACH + RIGHT_REACH) * size, width), f32),
             pltpu.VMEM((1, blocks * size), f32),
             pltpu.VMEM((1, blocks * size), f32),
-            pltpu.SemaphoreType.DMA((16 + 2 * ITERS,)),
-            pltpu.SemaphoreType.DMA((16 + 2 * ITERS,)),
+            pltpu.SemaphoreType.DMA((16 + 4 * ITERS,)),
+            pltpu.SemaphoreType.DMA((16 + 4 * ITERS,)),
             pltpu.SemaphoreType.DMA((5,)),
         ],
         compiler_params=pltpu.CompilerParams(

time: 54 us -> 52.7 us (0.976)
  Pallas kernels: 50.1 us -> 48.8 us
    pallas_call x1, Pallas kernels: 50.1 us -> 48.8 us  [columns_split(): pl.pallas_call(functools.partial(filter_kernel, rows_n), out_shape=(jax.S...]
where the time goes in v8:
time: 52.7 us; the launch traced here: 52.5 us
  Pallas kernels  48.8 us (93%)
  local copies, waits for them, and re-layouts  3.12 us (6%)
  between operations  0.64 us (1%)
    pallas_call x1, Pallas kernels, columns_split(): pl.pallas_call(functools.partial(filter_kernel, rows_n), out_shape=(jax.S...  48.8 us
    unnamed x2, local copies, waits for them, and re-layouts  3.12 us

profile of v8, /device:TPU:0, one launch (start us, length us, event | category | flops | bytes accessed | tf_op | source)
XLA Modules:
  0.0 52.5 jit_solution(6732956455124016412)
XLA Ops:
  0.6 48.8 %shard_map.68 = (f32[1024,128]{1,0:T(8,128)}, f32[1,512]{1,0:T(1,128)}) custom-call(f32[1024,128]{1,0:T(8,128)} %v_hbm.1, f32[4,8,128,128]{3,2,1,0:T(8,128)} %h_ref.1, s32[4,8]{1,0:T(4,128)} %colsh_ref.1, s32[1,4]{1,0:T(1,128)} %bitcast.3, s32[4,8]{1,0:T(4,128)} %colsh_ref.1, s32[1,4]{1,0:T(1,128)} %bitcast.4, f32[1,256]{1,0:T(1,128)} %bitcast.6), custom_call_target="tpu_custom_call" | custom-call | tf_op jit(solution)/shard_map/pallas_call | solution.py:441
  49.4 1.9 %copy.9 = f32[1024,128]{1,0:T(8,128)} copy(f32[1024,128]{1,0:T(8,128)} %get-tuple-element.8) | data formatting | bytes 1048576
  51.3 1.3 %copy.10 = f32[512]{0:T(512)} copy(f32[512]{0:T(512)} %bitcast.5) | data formatting | bytes 4096
